TPU v7x, 32 devices: a whole 2x2x4 slice. The times are simulated.
32 devices in a mesh: prow: 8 (over z, x), pcol: 2 (over y), zgrid: 2 (over core).
Axes of the slice: x: 2, y: 2, z: 4, core: 2. Of those that a mesh axis runs over, the one named last changes fastest.
Arguments:
- blocks: bfloat16 [8, 2, 2, 3, 40, 128, 128], P('prow', 'pcol', 'zgrid'), may hold values from -0.078125 to 0.078125
- sources: int32 [8, 2, 2, 3, 40], P('prow', 'pcol', 'zgrid'), may hold values from 0 to 1, as said below
- targets: int32 [8, 2, 2, 3, 40], P('prow', 'pcol', 'zgrid'), may hold values from 0 to 23, as said below
- counts: int32 [8, 2, 2, 3], P('prow', 'pcol', 'zgrid'), may hold values from 1 to 40, as said below
- given_sub: bfloat16 [8, 2, 2, 2, 128, 128], P('prow', 'pcol', 'zgrid'), may hold values from -6 to 6
- given_top: bfloat16 [8, 2, 2, 128, 128], P('prow', 'pcol'), may hold values from -6 to 6
- inverse_sub: bfloat16 [8, 2, 2, 2, 128, 128], P('prow', 'pcol', 'zgrid'), as said below
- inverse_top: bfloat16 [8, 2, 2, 128, 128], P('prow', 'pcol'), as said below
Outputs:
- solved_sub: bfloat16 [8, 2, 2, 2, 128, 128], P('prow', 'pcol', 'zgrid')
- solved_top: bfloat16 [8, 2, 2, 128, 128], P('prow', 'pcol')
Inputs may be any that keep to these rules, and one draw needn't show every extreme that they name: `sources`: column of the source supernode of a slot. `targets`: a slot of source level l aims at a level t = value // 8 + 1 above l and the row value % 8. `counts`: on some device of each source level all 40 slots are live. `inverse_sub`: unit lower triangular. `inverse_top`: unit lower triangular.
All inputs are finite; a program needn't handle non-finite values.
Results may differ from a plain program's by a relative error of at most 0.023.
Values may be sent and summed in bfloat16 or wider, within the bound.
No kernel may reach another device: no remote copies, remote signals or barrier semaphores. Data moves between devices by JAX's collectives and lax.ppermute only.
A program may use at most 64 MiB of HBM per device.

v0:
```python
import jax
import jax.numpy as jnp
from jax import lax
from jax.sharding import PartitionSpec as P

slot_group = 8


def solve_block(inverse, residual):
    return jnp.dot(inverse, residual, preferred_element_type=jnp.float32).astype(jnp.bfloat16)


def spread_updates(totals, solved, block_set, source_ids, target_ids, live_count):
    gathered = lax.all_gather(solved[None], "pcol", axis=0, tiled=True)
    group_count = (live_count + slot_group - 1) // slot_group

    def add_group(position, running):
        first_slot = position * slot_group
        block_piece = lax.dynamic_slice_in_dim(block_set, first_slot, slot_group, 0)
        source_part = lax.dynamic_slice_in_dim(source_ids, first_slot, slot_group, 0)
        target_part = lax.dynamic_slice_in_dim(target_ids, first_slot, slot_group, 0)
        chosen = jnp.take(gathered, source_part, axis=0)
        product = jnp.einsum(
            "swk,skr->swr", block_piece, chosen, preferred_element_type=jnp.float32
        )
        alive_mask = first_slot + jnp.arange(slot_group) < live_count
        product = product * alive_mask.astype(jnp.float32)[:, None, None]
        return running.at[target_part].add(product)

    return lax.fori_loop(0, group_count, add_group, totals)


def reduce_rows(totals, level_index, row_count):
    section = lax.slice_in_dim(
        totals, level_index * row_count, (level_index + 1) * row_count, axis=0
    )
    return lax.psum_scatter(
        section.astype(jnp.bfloat16), "prow", scatter_dimension=0, tiled=True
    ).astype(jnp.float32)[0]


def ancestor_solve(incoming, given, inverse):
    merged = lax.psum(incoming.astype(jnp.bfloat16), "zgrid").astype(jnp.float32)
    residual = (given.astype(jnp.float32) - merged).astype(jnp.bfloat16)
    return solve_block(inverse, residual)


def local(blocks, sources, targets, counts, given_sub, given_top, inverse_sub, inverse_top):
    block_set = blocks[0, 0, 0]
    source_ids = sources[0, 0, 0]
    target_ids = targets[0, 0, 0]
    live_counts = counts[0, 0, 0]
    right_sub = given_sub[0, 0, 0]
    right_top = given_top[0, 0]
    factor_sub = inverse_sub[0, 0, 0]
    factor_top = inverse_top[0, 0]
    row_count = lax.axis_size("prow")
    totals = jnp.zeros((3 * row_count,) + right_sub.shape[1:], jnp.float32)
    level_zero = solve_block(factor_sub[0], right_sub[0])
    totals = spread_updates(
        totals, level_zero, block_set[0], source_ids[0], target_ids[0], live_counts[0]
    )
    incoming = reduce_rows(totals, 0, row_count)
    level_one = solve_block(
        factor_sub[1], (right_sub[1].astype(jnp.float32) - incoming).astype(jnp.bfloat16)
    )
    totals = spread_updates(
        totals, level_one, block_set[1], source_ids[1], target_ids[1], live_counts[1]
    )
    level_two = ancestor_solve(reduce_rows(totals, 1, row_count), right_top[0], factor_top[0])
    totals = spread_updates(
        totals, level_two, block_set[2], source_ids[2], target_ids[2], live_counts[2]
    )
    level_three = ancestor_solve(reduce_rows(totals, 2, row_count), right_top[1], factor_top[1])
    solved_sub = jnp.stack([level_zero, level_one])[None, None, None]
    solved_top = jnp.stack([level_two, level_three])[None, None]
    return (solved_sub, solved_top)


def solution(mesh):
    in_specs = (
        P("prow", "pcol", "zgrid", None, None, None, None),
        P("prow", "pcol", "zgrid", None, None),
        P("prow", "pcol", "zgrid", None, None),
        P("prow", "pcol", "zgrid", None),
        P("prow", "pcol", "zgrid", None, None, None),
        P("prow", "pcol", None, None, None),
        P("prow", "pcol", "zgrid", None, None, None),
        P("prow", "pcol", None, None, None),
    )
    out_specs = (P("prow", "pcol", "zgrid", None, None, None), P("prow", "pcol", None, None, None))
    return jax.shard_map(local, mesh=mesh, in_specs=in_specs, out_specs=out_specs, check_vma=False)
```

profile of v0, /device:TPU:0, one launch (start us, length us, event | category | flops | bytes accessed | tf_op | source)
XLA Modules:
  0.0 280.8 jit_solution(14573704317749969175)
XLA Ops:
  7.2 1.4 fusion.42
  9.3 4.2 %slice_bitcast_fusion = (bf16[40,128,128]{2,1,0:T(8,128)(2,1)}, bf16[40,128,128]{2,1,0:T(8,128)(2,1)}, bf16[40,128,128]{2,1,0:T(8,128)(2,1)}) fusion(bf16[1,1,1,3,40,128,128]{6,5,4,3,2,1,0:T(8,128)(2,1)} %param.16), kind=kLoop, calls=%fused_computation.42 | loop fusion | bytes 7864320 | tf_op jit(solution)/shard_map/squeeze | solution.py:72
  13.6 5.5 %all-gather = bf16[256,128]{1,0:T(8,128)(2,1)S(1)} all-gather(bf16[128,128]{1,0:T(8,128)(2,1)S(1)} %convolution_convert_fusion.3), channel_id=2, replica_groups=mesh['prow'=8,'pcol'=2,'zgrid'=2] {'pcol'}, dimensions={0}, use_global_device_ids=true | all-gather | bytes 98304 | tf_op jit(solution)/shard_map/all_gather | solution.py:14
  19.3 7.5 %while.30 = (s32[]{:T(128)}, f32[24,128,128]{2,1,0:T(8,128)S(1)}, s32[]{:T(128)}, s32[40]{0:T(128)S(1)}, bf16[40,128,128]{2,1,0:T(8,128)(2,1)}, /*index=5*/s32[4...) while((s32[]{:T(128)}, f32[24,128,128]{2,1,0:T(8,128)S(1)}, ...), condition=%wide.region_2.4_spmd, body=%wide.region_0.3_spmd.sunk | while | flops 33948772 | bytes 3150311 | solution.py:30
  20.7 1.3 convolution_multiply_fusion.6
  22.0 1.0 scatter_fusion
  24.4 1.3 convolution_multiply_fusion.6
  25.7 1.0 scatter_fusion
  28.3 70.8 %reduce-scatter.4.cloned.1.call-done = bf16[1,128,128]{2,1,0:T(8,128)(2,1)} async-done(((bf16[8,128,128]{2,1,0:T(8,128)(2,1)}), bf16[1,128,128]{2,1,0:T(8,128)(2,1)}) %reduce-scatter.4.cloned.1.call-update) | async-done | bytes 32784 | tf_op jit(solution)/shard_map/reduce_scatter | solution.py:37
  99.9 4.6 %all-gather.1 = bf16[256,128]{1,0:T(8,128)(2,1)S(1)} all-gather(bf16[128,128]{1,0:T(8,128)(2,1)S(1)} %bitcast.81), channel_id=3, replica_groups=mesh['prow'=8,'pcol'=2,'zgrid'=2] {'pcol'}, dimensions={0}, use_global_device_ids=true | all-gather | bytes 98304 | tf_op jit(solution)/shard_map/all_gather | solution.py:14
  104.5 7.4 %while.31 = (s32[]{:T(128)}, f32[24,128,128]{2,1,0:T(8,128)S(1)}, s32[]{:T(128)}, s32[40]{0:T(128)S(1)}, bf16[40,128,128]{2,1,0:T(8,128)(2,1)}, /*index=5*/s32[4...) while((s32[]{:T(128)}, f32[24,128,128]{2,1,0:T(8,128)S(1)}, ...), condition=%wide.region_6.8_spmd, body=%wide.region_4.7_spmd.sunk | while | flops 33948772 | bytes 3150311 | solution.py:30
  105.8 1.3 convolution_multiply_fusion.7
  107.2 1.0 scatter_fusion.1
  109.5 1.3 convolution_multiply_fusion.7
  113.4 66.9 %reduce-scatter.6.cloned.1.call-done = bf16[1,128,128]{2,1,0:T(8,128)(2,1)} async-done(((bf16[8,128,128]{2,1,0:T(8,128)(2,1)}), bf16[1,128,128]{2,1,0:T(8,128)(2,1)}) %reduce-scatter.6.cloned.1.call-update) | async-done | bytes 32784 | tf_op jit(solution)/shard_map/reduce_scatter | solution.py:37
  180.4 4.0 %psum.14 = bf16[128,128]{1,0:T(8,128)(2,1)S(1)} all-reduce(bf16[128,128]{1,0:T(8,128)(2,1)} %bitcast.85), channel_id=1, replica_groups=mesh['prow'=8,'pcol'=2,'zgrid'=2] {'zgrid'}, use_global_device_ids=true, to_apply=%region_8.10 | all-reduce | flops 16384 | bytes 65536 | tf_op jit(solution)/shard_map/psum | solution.py:43
  184.6 4.6 %all-gather.2 = bf16[256,128]{0,1:T(8,128)(2,1)S(1)} all-gather(bf16[128,128]{0,1:T(8,128)(2,1)S(1)} %bitcast.83), channel_id=4, replica_groups=mesh['prow'=8,'pcol'=2,'zgrid'=2] {'pcol'}, dimensions={0}, use_global_device_ids=true | all-gather | bytes 98304 | tf_op jit(solution)/shard_map/all_gather | solution.py:14
  189.4 15.0 %while.32 = (s32[]{:T(128)}, f32[24,128,128]{2,1,0:T(8,128)S(1)}, s32[]{:T(128)}, s32[40]{0:T(128)S(1)}, bf16[40,128,128]{2,1,0:T(8,128)(2,1)}, /*index=5*/s32[4...) while((s32[]{:T(128)}, f32[24,128,128]{2,1,0:T(8,128)S(1)}, ...), condition=%wide.region_11.13_spmd, body=%wide.region_9.12_spmd.sunk | while | flops 33948772 | bytes 3150311 | solution.py:30
  190.7 1.3 convolution_multiply_fusion.8
  194.5 1.3 convolution_multiply_fusion.8
  198.2 1.3 convolution_multiply_fusion.8
  202.0 1.3 convolution_multiply_fusion.8
  205.8 63.5 %reduce-scatter.8.cloned.1.call-done = bf16[1,128,128]{2,1,0:T(8,128)(2,1)} async-done(((bf16[8,128,128]{2,1,0:T(8,128)(2,1)}), bf16[1,128,128]{2,1,0:T(8,128)(2,1)}) %reduce-scatter.8.cloned.1.call-update) | async-done | bytes 32784 | tf_op jit(solution)/shard_map/reduce_scatter | solution.py:37
  269.2 4.0 %psum.15 = bf16[128,128]{1,0:T(8,128)(2,1)S(1)} all-reduce(bf16[128,128]{1,0:T(8,128)(2,1)} %bitcast.86), channel_id=1, replica_groups=mesh['prow'=8,'pcol'=2,'zgrid'=2] {'zgrid'}, use_global_device_ids=true, to_apply=%region_13.15 | all-reduce | flops 16384 | bytes 65536 | tf_op jit(solution)/shard_map/psum | solution.py:43
  (68 shorter events, 21.9 us)
Async XLA Ops:
  7.2 91.9 %reduce-scatter.4.cloned.1.call-start = ((), (), s32[]{:S(2)}) async-start(), calls=%async_computation.3 | async-start | bytes 294912 | tf_op jit(solution)/shard_map/reduce_scatter | solution.py:37
  9.2 4.3 %copy-start = (bf16[1,1,1,2,128,128]{5,4,3,2,1,0:T(8,128)(2,1)S(1)}, bf16[1,1,1,2,128,128]{5,4,3,2,1,0:T(8,128)(2,1)}, u32[]{:S(2)}) copy-start(bf16[1,1,1,2,128,128]{5,4,3,2,1,0:T(8,128)(2,1)} %param.20) | copy-start | bytes 196612
  9.3 4.3 %copy-start.1 = (bf16[1,1,1,2,128,128]{5,4,3,2,1,0:T(8,128)(2,1)S(1)}, bf16[1,1,1,2,128,128]{5,4,3,2,1,0:T(8,128)(2,1)}, u32[]{:S(2)}) copy-start(bf16[1,1,1,2,128,128]{5,4,3,2,1,0:T(8,128)(2,1)} %param.22) | copy-start | bytes 196612
  9.3 9.9 %copy-start.4 = (s32[1,1,1,3,40]{4,2,3,1,0:T(1,128)S(1)}, s32[1,1,1,3,40]{4,2,3,1,0:T(1,128)}, u32[]{:S(2)}) copy-start(s32[1,1,1,3,40]{4,2,3,1,0:T(1,128)} %param.17) | copy-start | bytes 1444
  9.3 9.9 %copy-start.5 = (s32[1,1,1,3,40]{4,2,3,1,0:T(1,128)S(1)}, s32[1,1,1,3,40]{4,2,3,1,0:T(1,128)}, u32[]{:S(2)}) copy-start(s32[1,1,1,3,40]{4,2,3,1,0:T(1,128)} %param.18) | copy-start | bytes 1444
  27.6 152.8 %reduce-scatter.6.cloned.1.call-start = ((), (), s32[]{:S(2)}) async-start(), calls=%async_computation.4 | async-start | bytes 294912 | tf_op jit(solution)/shard_map/reduce_scatter | solution.py:37
  104.5 79.9 %copy-start.2 = (bf16[1,1,2,128,128]{4,3,2,1,0:T(8,128)(2,1)S(1)}, bf16[1,1,2,128,128]{4,3,2,1,0:T(8,128)(2,1)}, u32[]{:S(2)}) copy-start(bf16[1,1,2,128,128]{4,3,2,1,0:T(8,128)(2,1)} %param.23) | copy-start | bytes 196612
  104.5 79.9 %copy-start.3 = (bf16[1,1,2,128,128]{4,3,2,1,0:T(8,128)(2,1)S(1)}, bf16[1,1,2,128,128]{4,3,2,1,0:T(8,128)(2,1)}, u32[]{:S(2)}) copy-start(bf16[1,1,2,128,128]{4,3,2,1,0:T(8,128)(2,1)} %param.21) | copy-start | bytes 196612
  112.7 156.5 %reduce-scatter.8.cloned.1.call-start = ((), (), s32[]{:S(2)}) async-start(), calls=%async_computation.5 | async-start | bytes 294912 | tf_op jit(solution)/shard_map/reduce_scatter | solution.py:37
Sparse Core Ops, SparseCore 0:
  27.7 71.2 reduce-scatter.3
  112.8 67.4 reduce-scatter.5
  205.2 63.9 reduce-scatter.7
where the time goes:
time: 283 us; the launch traced here: 281 us
  waiting for transfers between devices  201 us (71%)
  blocking collectives  22.8 us (8%)
  between operations  15.8 us (6%)
  other arithmetic  15.3 us (5%)
  local copies, waits for them, and re-layouts  13.7 us (5%)
  matrix products  11.4 us (4%)
    reduce_scatter x3, waiting for transfers between devices, reduce_rows(): lax.psum_scatter(section.astype(jnp.bfloat16), 'prow', scatter_dimension=...  201 us
    all_gather x3, blocking collectives, spread_updates(): gathered = lax.all_gather(solved[None], 'pcol', axis=0, tiled=True)  14.7 us
    dot_general x8, matrix products, add_group(): jnp.einsum('swk,skr->swr', block_piece, chosen, preferred_element_type=jn...  10 us
    scatter-add x8, other arithmetic, add_group(): return running.at[target_part].add(product)  8.25 us
    psum x2, blocking collectives, ancestor_solve(): lax.psum(incoming.astype(jnp.bfloat16), 'zgrid').astype(jnp.float32)  8.08 us
    and x8, other arithmetic, add_group(): chosen = jnp.take(gathered, source_part, axis=0)  5.75 us
  transfers between devices with their start and end apart: 3, of which 3 were waited for; matrix products, arithmetic and copies ran while one was open for 0% of the time, Pallas kernels for 0%

commit v1 on v0

--- a/solution.py
+++ b/solution.py
@@ -34,14 +34,22 @@
     section = lax.slice_in_dim(
         totals, level_index * row_count, (level_index + 1) * row_count, axis=0
     )
-    return lax.psum_scatter(
-        section.astype(jnp.bfloat16), "prow", scatter_dimension=0, tiled=True
-    ).astype(jnp.float32)[0]
+    received = lax.all_to_all(section.astype(jnp.bfloat16), "prow", 0, 0, tiled=True)
+    return jnp.sum(received.astype(jnp.float32), axis=0)
+
+
+def reduce_all(totals, level_index, row_count):
+    section = lax.slice_in_dim(
+        totals, level_index * row_count, (level_index + 1) * row_count, axis=0
+    ).astype(jnp.bfloat16)
+    layer_count = lax.axis_size("zgrid")
+    copies = jnp.repeat(section, layer_count, axis=0)
+    received = lax.all_to_all(copies, ("prow", "zgrid"), 0, 0, tiled=True)
+    return jnp.sum(received.astype(jnp.float32), axis=0)
 
 
 def ancestor_solve(incoming, given, inverse):
-    merged = lax.psum(incoming.astype(jnp.bfloat16), "zgrid").astype(jnp.float32)
-    residual = (given.astype(jnp.float32) - merged).astype(jnp.bfloat16)
+    residual = (given.astype(jnp.float32) - incoming).astype(jnp.bfloat16)
     return solve_block(inverse, residual)
 
 
@@ -67,11 +75,11 @@
     totals = spread_updates(
         totals, level_one, block_set[1], source_ids[1], target_ids[1], live_counts[1]
     )
-    level_two = ancestor_solve(reduce_rows(totals, 1, row_count), right_top[0], factor_top[0])
+    level_two = ancestor_solve(reduce_all(totals, 1, row_count), right_top[0], factor_top[0])
     totals = spread_updates(
         totals, level_two, block_set[2], source_ids[2], target_ids[2], live_counts[2]
     )
-    level_three = ancestor_solve(reduce_rows(totals, 2, row_count), right_top[1], factor_top[1])
+    level_three = ancestor_solve(reduce_all(totals, 2, row_count), right_top[1], factor_top[1])
     solved_sub = jnp.stack([level_zero, level_one])[None, None, None]
     solved_top = jnp.stack([level_two, level_three])[None, None]
     return (solved_sub, solved_top)

time: 283 us -> 132 us (0.47)
  waiting for transfers between devices: 201 us -> 36.8 us
  starting transfers between devices: 0.12 us -> 40.4 us
  between operations: 15.8 us -> 2.7 us
  blocking collectives: 22.8 us -> 14.7 us
    reduce_scatter x3 -> x0, waiting for transfers between devices: 201 us -> none  [reduce_rows(): lax.psum_scatter(section.astype(jnp.bfloat16), 'prow', scatter_dimension=...]
    all_to_all x0 -> x3, starting transfers between devices: none -> 40.4 us  [the longest x2 21.3 us: reduce_all(): received = lax.all_to_all(copies, ('prow', 'zgrid'), 0, 0, tiled=True)]
    all_to_all x0 -> x3, waiting for transfers between devices: none -> 36.8 us  [the longest x2 27.6 us: reduce_all(): received = lax.all_to_all(copies, ('prow', 'zgrid'), 0, 0, tiled=True)]
    psum x2 -> x0, blocking collectives: 8.08 us -> none  [ancestor_solve(): lax.psum(incoming.astype(jnp.bfloat16), 'zgrid').astype(jnp.float32)]
    dot_general x8 -> x7, matrix products: 10 us -> 8.76 us  [add_group(): jnp.einsum('swk,skr->swr', block_piece, chosen, preferred_element_type=jn...]
    and x8 -> x7, other arithmetic: 5.75 us -> 4.62 us  [add_group(): chosen = jnp.take(gathered, source_part, axis=0)]
    scatter-add x8 -> x7, other arithmetic: 8.25 us -> 7.22 us  [add_group(): return running.at[target_part].add(product)]
where the time goes in v1:
time: 132 us; the launch traced here: 131 us
  starting transfers between devices  40.4 us (31%)
  waiting for transfers between devices  36.8 us (28%)
  blocking collectives  14.7 us (11%)
  local copies, waits for them, and re-layouts  13.4 us (10%)
  other arithmetic  13.3 us (10%)
  matrix products  9.39 us (7%)
  between operations  2.7 us (2%)
    all_to_all x2, waiting for transfers between devices, reduce_all(): received = lax.all_to_all(copies, ('prow', 'zgrid'), 0, 0, tiled=True)  27.6 us
    all_to_all x2, starting transfers between devices, reduce_all(): received = lax.all_to_all(copies, ('prow', 'zgrid'), 0, 0, tiled=True)  21.3 us
    all_to_all x1, starting transfers between devices, reduce_rows(): lax.all_to_all(section.astype(jnp.bfloat16), 'prow', 0, 0, tiled=True)  19.2 us
    all_gather x3, blocking collectives, spread_updates(): gathered = lax.all_gather(solved[None], 'pcol', axis=0, tiled=True)  14.7 us
    all_to_all x1, waiting for transfers between devices, reduce_rows(): lax.all_to_all(section.astype(jnp.bfloat16), 'prow', 0, 0, tiled=True)  9.22 us
    dot_general x7, matrix products, add_group(): jnp.einsum('swk,skr->swr', block_piece, chosen, preferred_element_type=jn...  8.76 us
    scatter-add x7, other arithmetic, add_group(): return running.at[target_part].add(product)  7.22 us
    and x7, other arithmetic, add_group(): chosen = jnp.take(gathered, source_part, axis=0)  4.62 us
  transfers between devices with their start and end apart: 3, of which 3 were waited for; matrix products, arithmetic and copies ran while one was open for 0% of the time, Pallas kernels for 0%

profile of v1, /device:TPU:0, one launch (start us, length us, event | category | flops | bytes accessed | tf_op | source)
XLA Modules:
  0.0 131.1 jit_solution(17870355940915025098)
XLA Ops:
  0.6 1.4 %fusion.41 = (s32[1,1,1,1]{3,2,1,0:T(1,128)}, s32[1,1,1,1]{3,2,1,0:T(1,128)}, s32[1,1,1,1]{3,2,1,0:T(1,128)}) fusion(s32[1,1,1,3]{3,2,1,0:T(1,128)} %param.19), kind=kLoop, calls=%fused_computation.86 | loop fusion | bytes 24 | tf_op jit(solution)/shard_map/slice | solution.py:80
  2.7 4.2 %slice_bitcast_fusion = (bf16[40,128,128]{2,1,0:T(8,128)(2,1)}, bf16[40,128,128]{2,1,0:T(8,128)(2,1)}, bf16[40,128,128]{2,1,0:T(8,128)(2,1)}) fusion(bf16[1,1,1,3,40,128,128]{6,5,4,3,2,1,0:T(8,128)(2,1)} %param.16), kind=kLoop, calls=%fused_computation.42 | loop fusion | bytes 7864320 | tf_op jit(solution)/shard_map/squeeze | solution.py:80
  7.0 5.5 %all-gather = bf16[256,128]{1,0:T(8,128)(2,1)S(1)} all-gather(bf16[128,128]{1,0:T(8,128)(2,1)S(1)} %convolution_convert_fusion.3), channel_id=2, replica_groups=mesh['prow'=8,'pcol'=2,'zgrid'=2] {'pcol'}, dimensions={0}, use_global_device_ids=true | all-gather | bytes 98304 | tf_op jit(solution)/shard_map/all_gather | solution.py:14
  12.7 3.7 %while.30 = (s32[]{:T(128)}, f32[24,128,128]{2,1,0:T(8,128)S(1)}, s32[]{:T(128)}, s32[40]{0:T(128)S(1)}, bf16[40,128,128]{2,1,0:T(8,128)(2,1)}, /*index=5*/s32[4...) while((s32[]{:T(128)}, f32[24,128,128]{2,1,0:T(8,128)S(1)}, ...), condition=%wide.region_2.4_spmd, body=%wide.region_0.3_spmd.sunk | while | flops 33948772 | bytes 3150311 | solution.py:30
  14.0 1.3 convolution_multiply_fusion.6
  15.4 1.0 scatter_fusion
  17.2 19.2 %all-to-all-start = ((bf16[8,128,128]{2,1,0:T(8,128)(2,1)}), bf16[8,128,128]{2,1,0:T(8,128)(2,1)S(1)}, u32[]{:S(2)}, u32[]{:S(2)}) async-start(bf16[8,128,128]{2,1,0:T(8,128)(2,1)} %slice.170), calls=%async_computation | async-start | bytes 524288 | tf_op jit(solution)/shard_map/all_to_all | solution.py:37
  36.9 9.2 %all-to-all-done = bf16[8,128,128]{2,1,0:T(8,128)(2,1)S(1)} async-done(((bf16[8,128,128]{2,1,0:T(8,128)(2,1)}), bf16[8,128,128]{2,1,0:T(8,128)(2,1)S(1)}, u32[]{:S(2)}, u32[]{:S(2)}) %all-to-all-start) | async-done | bytes 262176 | tf_op jit(solution)/shard_map/all_to_all | solution.py:37
  46.3 4.6 %all-gather.1 = bf16[256,128]{1,0:T(8,128)(2,1)S(1)} all-gather(bf16[128,128]{1,0:T(8,128)(2,1)S(1)} %bitcast.90), channel_id=3, replica_groups=mesh['prow'=8,'pcol'=2,'zgrid'=2] {'pcol'}, dimensions={0}, use_global_device_ids=true | all-gather | bytes 98304 | tf_op jit(solution)/shard_map/all_gather | solution.py:14
  50.9 18.2 %while.31 = (s32[]{:T(128)}, f32[24,128,128]{2,1,0:T(8,128)S(1)}, s32[]{:T(128)}, s32[40]{0:T(128)S(1)}, bf16[40,128,128]{2,1,0:T(8,128)(2,1)}, /*index=5*/s32[4...) while((s32[]{:T(128)}, f32[24,128,128]{2,1,0:T(8,128)S(1)}, ...), condition=%wide.region_6.8_spmd, body=%wide.region_4.7_spmd.sunk | while | flops 33948772 | bytes 3150311 | solution.py:30
  52.1 1.3 convolution_multiply_fusion.7
  55.8 1.3 convolution_multiply_fusion.7
  59.4 1.3 convolution_multiply_fusion.7
  63.1 1.3 convolution_multiply_fusion.7
  64.4 1.0 scatter_fusion.1
  66.8 1.3 convolution_multiply_fusion.7
  68.1 1.0 scatter_fusion.1
  70.1 3.6 %all-to-all-start.1 = ((bf16[16,128,128]{2,1,0:T(8,128)(2,1)}), bf16[16,128,128]{2,1,0:T(8,128)(2,1)S(1)}, u32[]{:S(2)}, u32[]{:S(2)}) async-start(bf16[16,128,128]{2,1,0:T(8,128)(2,1)} %bitcast.19), calls=%async_computation.1 | async-start | bytes 1048576 | tf_op jit(solution)/shard_map/all_to_all | solution.py:47
  74.4 13.8 %all-to-all-done.1 = bf16[16,128,128]{2,1,0:T(8,128)(2,1)S(1)} async-done(((bf16[16,128,128]{2,1,0:T(8,128)(2,1)}), bf16[16,128,128]{2,1,0:T(8,128)(2,1)S(1)}, u32[]{:S(2)}, u32[]{:S(2)}) %all-to-all-start.1) | async-done | bytes 524320 | tf_op jit(solution)/shard_map/all_to_all | solution.py:47
  88.4 4.6 %all-gather.2 = bf16[256,128]{0,1:T(8,128)(2,1)S(1)} all-gather(bf16[128,128]{0,1:T(8,128)(2,1)S(1)} %bitcast.92), channel_id=4, replica_groups=mesh['prow'=8,'pcol'=2,'zgrid'=2] {'pcol'}, dimensions={0}, use_global_device_ids=true | all-gather | bytes 98304 | tf_op jit(solution)/shard_map/all_gather | solution.py:14
  93.2 3.7 %while.32 = (s32[]{:T(128)}, f32[24,128,128]{2,1,0:T(8,128)S(1)}, s32[]{:T(128)}, s32[40]{0:T(128)S(1)}, bf16[40,128,128]{2,1,0:T(8,128)(2,1)}, /*index=5*/s32[4...) while((s32[]{:T(128)}, f32[24,128,128]{2,1,0:T(8,128)S(1)}, ...), condition=%wide.region_10.12_spmd, body=%wide.region_8.11_spmd.sunk | while | flops 33948772 | bytes 3150311 | solution.py:30
  94.5 1.3 convolution_multiply_fusion.8
  97.9 17.7 %all-to-all-start.2 = ((bf16[16,128,128]{2,1,0:T(8,128)(2,1)}), bf16[16,128,128]{2,1,0:T(8,128)(2,1)S(1)}, u32[]{:S(2)}, u32[]{:S(2)}) async-start(bf16[16,128,128]{2,1,0:T(8,128)(2,1)} %bitcast.30), calls=%async_computation.2 | async-start | bytes 1048576 | tf_op jit(solution)/shard_map/all_to_all | solution.py:47
  116.2 13.8 %all-to-all-done.2 = bf16[16,128,128]{2,1,0:T(8,128)(2,1)S(1)} async-done(((bf16[16,128,128]{2,1,0:T(8,128)(2,1)}), bf16[16,128,128]{2,1,0:T(8,128)(2,1)S(1)}, u32[]{:S(2)}, u32[]{:S(2)}) %all-to-all-start.2) | async-done | bytes 524320 | tf_op jit(solution)/shard_map/all_to_all | solution.py:47
  (62 shorter events, 18.7 us)
Async XLA Ops:
  2.6 4.2 %copy-start = (bf16[1,1,1,2,128,128]{5,4,3,2,1,0:T(8,128)(2,1)S(1)}, bf16[1,1,1,2,128,128]{5,4,3,2,1,0:T(8,128)(2,1)}, u32[]{:S(2)}) copy-start(bf16[1,1,1,2,128,128]{5,4,3,2,1,0:T(8,128)(2,1)} %param.20) | copy-start | bytes 196612
  2.6 4.2 %copy-start.1 = (bf16[1,1,1,2,128,128]{5,4,3,2,1,0:T(8,128)(2,1)S(1)}, bf16[1,1,1,2,128,128]{5,4,3,2,1,0:T(8,128)(2,1)}, u32[]{:S(2)}) copy-start(bf16[1,1,1,2,128,128]{5,4,3,2,1,0:T(8,128)(2,1)} %param.22) | copy-start | bytes 196612
  2.6 9.9 %copy-start.4 = (s32[1,1,1,3,40]{4,2,3,1,0:T(1,128)S(1)}, s32[1,1,1,3,40]{4,2,3,1,0:T(1,128)}, u32[]{:S(2)}) copy-start(s32[1,1,1,3,40]{4,2,3,1,0:T(1,128)} %param.17) | copy-start | bytes 1444
  2.7 9.9 %copy-start.5 = (s32[1,1,1,3,40]{4,2,3,1,0:T(1,128)S(1)}, s32[1,1,1,3,40]{4,2,3,1,0:T(1,128)}, u32[]{:S(2)}) copy-start(s32[1,1,1,3,40]{4,2,3,1,0:T(1,128)} %param.18) | copy-start | bytes 1444
  17.2 29.0 %all-to-all-start = ((bf16[8,128,128]{2,1,0:T(8,128)(2,1)}), bf16[8,128,128]{2,1,0:T(8,128)(2,1)S(1)}, u32[]{:S(2)}, u32[]{:S(2)}) async-start(bf16[8,128,128]{2,1,0:T(8,128)(2,1)} %slice.170), calls=%async_computation | async-start | bytes 524288 | tf_op jit(solution)/shard_map/all_to_all | solution.py:37
  69.1 19.1 %copy-start.2 = (bf16[1,1,2,128,128]{4,3,2,1,0:T(8,128)(2,1)S(1)}, bf16[1,1,2,128,128]{4,3,2,1,0:T(8,128)(2,1)}, u32[]{:S(2)}) copy-start(bf16[1,1,2,128,128]{4,3,2,1,0:T(8,128)(2,1)} %param.23) | copy-start | bytes 196612
  69.2 19.1 %copy-start.3 = (bf16[1,1,2,128,128]{4,3,2,1,0:T(8,128)(2,1)S(1)}, bf16[1,1,2,128,128]{4,3,2,1,0:T(8,128)(2,1)}, u32[]{:S(2)}) copy-start(bf16[1,1,2,128,128]{4,3,2,1,0:T(8,128)(2,1)} %param.21) | copy-start | bytes 196612
  70.1 18.0 %all-to-all-start.1 = ((bf16[16,128,128]{2,1,0:T(8,128)(2,1)}), bf16[16,128,128]{2,1,0:T(8,128)(2,1)S(1)}, u32[]{:S(2)}, u32[]{:S(2)}) async-start(bf16[16,128,128]{2,1,0:T(8,128)(2,1)} %bitcast.19), calls=%async_computation.1 | async-start | bytes 1048576 | tf_op jit(solution)/shard_map/all_to_all | solution.py:47
  97.9 32.2 %all-to-all-start.2 = ((bf16[16,128,128]{2,1,0:T(8,128)(2,1)}), bf16[16,128,128]{2,1,0:T(8,128)(2,1)S(1)}, u32[]{:S(2)}, u32[]{:S(2)}) async-start(bf16[16,128,128]{2,1,0:T(8,128)(2,1)} %bitcast.30), calls=%async_computation.2 | async-start | bytes 1048576 | tf_op jit(solution)/shard_map/all_to_all | solution.py:47

commit v2 on v0

v2 whole, which is shorter than its diff:
```python
import functools

import jax
import jax.numpy as jnp
from jax import lax
from jax.experimental import pallas as pl
from jax.experimental.pallas import tpu as pltpu
from jax.sharding import PartitionSpec as P

slot_group = 8


def shifted_copies(value, layers):
    cols = lax.axis_size("pcol")
    depth = lax.axis_size("zgrid")
    found = []
    for k in range(cols):
        if k == 0 and layers == 0:
            found.append(value)
            continue
        moves = []
        for c in range(cols):
            for z in range(depth):
                target = ((c - k) % cols) * depth + (z - layers) % depth
                moves.append((c * depth + z, target))
        found.append(lax.ppermute(value, ("pcol", "zgrid"), moves))
    return found


def from_other_core(value, shift):
    depth = lax.axis_size("zgrid")
    return lax.ppermute(value, "zgrid", [(z, (z - shift) % depth) for z in range(depth)])


def update_kernel(sets, cols, row_count, lowest_kept, carries, keeps, *refs):
    refs = list(refs)
    set_count = len(sets)
    solution_sets = 1 + max(s[2] for s in sets)
    layer_sets = 1 + max(s[3] for s in sets)
    metas = [[refs.pop(0) for _ in range(4)] for _ in range(layer_sets)]
    solutions = [[refs.pop(0) for _ in range(cols)] for _ in range(solution_sets)]
    total_in = refs.pop(0) if carries else None
    send_ref = refs.pop(0) if keeps[0] else None
    kept_ref = refs.pop(0) if keeps[1] else None
    buffer, wide, product, total, semaphores = refs
    me = lax.axis_index("pcol")
    capacity = buffer.shape[1]
    width = buffer.shape[2]
    groups = capacity // slot_group

    def group_copy(k, g):
        level = sets[k][0]
        blocks = metas[sets[k][3]][3]
        return pltpu.make_async_copy(
            blocks.at[level, pl.ds(g * slot_group, slot_group)],
            buffer.at[k, pl.ds(g * slot_group, slot_group)],
            semaphores.at[k, g],
        )

    for k in range(set_count):
        live = metas[sets[k][3]][2][sets[k][0]]
        for g in range(groups):

            @pl.when(g * slot_group < live)
            def _():
                group_copy(k, g).start()

    if carries:
        total[: total_in.shape[0]] = total_in[...]
    else:
        total[...] = jnp.zeros_like(total)
    spare = total.shape[0] - 1
    for j in range(solution_sets):
        for c in range(cols):
            wide[j, :, c * width : (c + 1) * width] = solutions[j][c][...]

    for k in range(set_count):
        level, lowest, solution_index, layer_index = sets[k]
        sources, targets, counts, _ = metas[layer_index]
        live = counts[level]

        def one_group(g, unused):
            group_copy(k, g).wait()
            first = g * slot_group
            pieces = buffer[k, pl.ds(first, slot_group)].reshape(slot_group * width, width)
            product[...] = jnp.dot(
                pieces, wide[solution_index], preferred_element_type=jnp.float32
            )
            for s in range(slot_group):
                slot = first + s
                aim = targets[level, slot] - lowest_kept * row_count
                used = (slot < live) & (targets[level, slot] >= lowest * row_count)
                place = jnp.where(used, aim, spare)
                column = lax.rem(sources[level, slot] - me + cols, cols)
                total[place] += product[
                    s * width : (s + 1) * width, pl.ds(pl.multiple_of(column * width, width), width)
                ]
            return unused

        lax.fori_loop(0, (live + slot_group - 1) // slot_group, one_group, 0)

    if keeps[0]:
        send_ref[...] = total[:row_count].astype(jnp.bfloat16)
    if keeps[1]:
        first = row_count if keeps[0] else 0
        kept_ref[...] = total[first:spare]


def update(sets, layer_arrays, solution_groups, total_in, row_count, lowest_kept, sends, keeps):
    cols = len(solution_groups[0])
    width, sides = solution_groups[0][0].shape
    capacity = layer_arrays[0][3].shape[1]
    sections = 3 - lowest_kept
    operands = []
    specs = []
    for sources, targets, counts, blocks in layer_arrays:
        operands += [sources, targets, counts, blocks]
        specs += [pl.BlockSpec(memory_space=pltpu.SMEM)] * 3 + [pl.BlockSpec(memory_space=pl.ANY)]
    for group in solution_groups:
        operands += group
        specs += [pl.BlockSpec(memory_space=pltpu.VMEM)] * cols
    if total_in is not None:
        operands.append(total_in)
        specs.append(pl.BlockSpec(memory_space=pltpu.VMEM))
    outs = []
    if sends:
        outs.append(jax.ShapeDtypeStruct((row_count, width, sides), jnp.bfloat16))
    if keeps:
        outs.append(
            jax.ShapeDtypeStruct(((sections - int(sends)) * row_count, width, sides), jnp.float32)
        )
    return pl.pallas_call(
        functools.partial(
            update_kernel, sets, cols, row_count, lowest_kept, total_in is not None, (sends, keeps)
        ),
        out_shape=outs,
        in_specs=specs,
        out_specs=[pl.BlockSpec(memory_space=pltpu.VMEM)] * len(outs),
        scratch_shapes=[
            pltpu.VMEM((len(sets), capacity, width, width), jnp.bfloat16),
            pltpu.VMEM((len(solution_groups), width, cols * sides), jnp.bfloat16),
            pltpu.VMEM((slot_group * width, cols * sides), jnp.float32),
            pltpu.VMEM((sections * row_count + 1, width, sides), jnp.float32),
            pltpu.SemaphoreType.DMA((len(sets), capacity // slot_group)),
        ],
        compiler_params=pltpu.CompilerParams(vmem_limit_bytes=48 * 1024 * 1024),
    )(*operands)


def solve_block(inverse, residual):
    return jnp.dot(inverse, residual, preferred_element_type=jnp.float32).astype(jnp.bfloat16)


def reduced_solve(send, given, inverse):
    received = lax.all_to_all(send, "prow", 0, 0, tiled=True)
    incoming = jnp.sum(received.astype(jnp.float32), axis=0)
    residual = (given.astype(jnp.float32) - incoming).astype(jnp.bfloat16)
    return solve_block(inverse, residual)


def local(blocks, sources, targets, counts, given_sub, given_top, inverse_sub, inverse_top):
    own = (sources[0, 0, 0], targets[0, 0, 0], counts[0, 0, 0], blocks[0, 0, 0])
    right_sub = given_sub[0, 0, 0]
    right_top = given_top[0, 0]
    factor_sub = inverse_sub[0, 0, 0]
    factor_top = inverse_top[0, 0]
    row_count = lax.axis_size("prow")
    depth = lax.axis_size("zgrid")
    others = [tuple(from_other_core(a, m) for a in own) for m in range(1, depth)]

    level_zero = solve_block(factor_sub[0], right_sub[0])
    spread_zero = [shifted_copies(level_zero, m) for m in range(depth)]
    send, total = update(
        [(0, 0, 0, 0)], [own], spread_zero[:1], None, row_count, 0, True, True
    )
    level_one = reduced_solve(send, right_sub[1], factor_sub[1])
    (total,) = update(
        [(0, 1, m, m) for m in range(depth - 1)],
        others, spread_zero[1:], total, row_count, 1, False, True,
    )
    spread_one = [shifted_copies(level_one, m) for m in range(depth)]
    send, total = update(
        [(1, 1, m, m) for m in range(depth)],
        [own] + others, spread_one, total, row_count, 1, True, True,
    )
    level_two = reduced_solve(send, right_top[0], factor_top[0])
    spread_two = shifted_copies(level_two, 0)
    (send,) = update(
        [(2, 2, 0, m) for m in range(depth)],
        [own] + others, [spread_two], total, row_count, 2, True, False,
    )
    level_three = reduced_solve(send, right_top[1], factor_top[1])
    solved_sub = jnp.stack([level_zero, level_one])[None, None, None]
    solved_top = jnp.stack([level_two, level_three])[None, None]
    return (solved_sub, solved_top)


def solution(mesh):
    in_specs = (
        P("prow", "pcol", "zgrid", None, None, None, None),
        P("prow", "pcol", "zgrid", None, None),
        P("prow", "pcol", "zgrid", None, None),
        P("prow", "pcol", "zgrid", None),
        P("prow", "pcol", "zgrid", None, None, None),
        P("prow", "pcol", None, None, None),
        P("prow", "pcol", "zgrid", None, None, None),
        P("prow", "pcol", None, None, None),
    )
    out_specs = (P("prow", "pcol", "zgrid", None, None, None), P("prow", "pcol", None, None, None))
    return jax.shard_map(local, mesh=mesh, in_specs=in_specs, out_specs=out_specs, check_vma=False)
```

time: 283 us -> 69.4 us (0.25)
  waiting for transfers between devices: 201 us -> 19 us
  starting transfers between devices: 0.12 us -> 17.6 us
  between operations: 15.8 us -> 0.81 us
  other arithmetic: 15.3 us -> 1.4 us
  Pallas kernels: 0 us -> 10.2 us
  matrix products: 11.4 us -> 1.3 us
  local copies, waits for them, and re-layouts: 13.7 us -> 4.16 us
  blocking collectives: 22.8 us -> 13.6 us
    reduce_scatter x3 -> x0, waiting for transfers between devices: 201 us -> none  [reduce_rows(): lax.psum_scatter(section.astype(jnp.bfloat16), 'prow', scatter_dimension=...]
    all_gather x3 -> x0, blocking collectives: 14.7 us -> none  [spread_updates(): gathered = lax.all_gather(solved[None], 'pcol', axis=0, tiled=True)]
    all_to_all x0 -> x2, waiting for transfers between devices: none -> 13.7 us  [reduced_solve(): received = lax.all_to_all(send, 'prow', 0, 0, tiled=True)]
    all_to_all x0 -> x1, blocking collectives: none -> 13.6 us  [reduced_solve(): received = lax.all_to_all(send, 'prow', 0, 0, tiled=True)]
    pallas_call x0 -> x4, Pallas kernels: none -> 10.2 us  [update(): pl.pallas_call(functools.partial(update_kernel, sets, cols, row_count, lo...]
    dot_general x8 -> x0, matrix products: 10 us -> none  [add_group(): jnp.einsum('swk,skr->swr', block_piece, chosen, preferred_element_type=jn...]
    all_to_all x0 -> x2, starting transfers between devices: none -> 9.83 us  [reduced_solve(): received = lax.all_to_all(send, 'prow', 0, 0, tiled=True)]
    scatter-add x8 -> x0, other arithmetic: 8.25 us -> none  [add_group(): return running.at[target_part].add(product)]
  transfers between devices with their start and end apart: 3 -> 13, of which waited for: 3 -> 5; matrix products, arithmetic and copies ran while one was open for 0% -> 5% of each run, Pallas kernels for 0% -> 6%
where the time goes in v2:
time: 69.4 us; the launch traced here: 68.1 us
  waiting for transfers between devices  19 us (27%)
  starting transfers between devices  17.6 us (25%)
  blocking collectives  13.6 us (20%)
  Pallas kernels  10.2 us (15%)
  local copies, waits for them, and re-layouts  4.16 us (6%)
  other arithmetic  1.4 us (2%)
  matrix products  1.3 us (2%)
  between operations  0.81 us (1%)
    all_to_all x2, waiting for transfers between devices, reduced_solve(): received = lax.all_to_all(send, 'prow', 0, 0, tiled=True)  13.7 us
    all_to_all x1, blocking collectives, reduced_solve(): received = lax.all_to_all(send, 'prow', 0, 0, tiled=True)  13.6 us
    pallas_call x4, Pallas kernels, update(): pl.pallas_call(functools.partial(update_kernel, sets, cols, row_count, lo...  10.2 us
    all_to_all x2, starting transfers between devices, reduced_solve(): received = lax.all_to_all(send, 'prow', 0, 0, tiled=True)  9.83 us
    ppermute x7, starting transfers between devices, shifted_copies(): found.append(lax.ppermute(value, ('pcol', 'zgrid'), moves))  6.57 us
    ppermute x7, waiting for transfers between devices, shifted_copies(): found.append(lax.ppermute(value, ('pcol', 'zgrid'), moves))  5.31 us
    unnamed x18, local copies, waits for them, and re-layouts  4.16 us
  transfers between devices with their start and end apart: 13, of which 5 were waited for; matrix products, arithmetic and copies ran while one was open for 5% of the time, Pallas kernels for 6%

profile of v2, /device:TPU:0, one launch (start us, length us, event | category | flops | bytes accessed | tf_op | source)
XLA Modules:
  0.0 68.1 jit_solution(8229615498083614405)
XLA Ops:
  0.7 0.5 collective-permute-start.4
  1.2 0.9 %convolution_convert_fusion.3.refs_4_ = bf16[128,128]{1,0:T(8,128)(2,1)S(1)} fusion(bf16[1,1,1,2,128,128]{5,4,3,2,1,0:T(8,128)(2,1)} %param.12, bf16[1,1,1,2,128,128]{5,4,3,2,1,0:T(8,128)(2,1)} %param.14), kind=kOutput, calls=%fused_computation.3 | convolution fusion | flops 4210688 | bytes 98304 | tf_op jit(solution)/shard_map/dot_general | solution.py:151
  2.1 2.6 %collective-permute-start = (bf16[128,128]{1,0:T(8,128)(2,1)S(1)}, bf16[128,128]{1,0:T(8,128)(2,1)S(1)}, u32[]{:S(2)}, u32[]{:S(2)}) collective-permute-start(bf16[128,128]{1,0:T(8,128)(2,1)S(1)} %convolution_convert_fusion.3.refs_4_), channel_id=1, source_target_pairs={{0,2},{1,3},{2,0},{3,1},{4,6},{5,7},{6,4},{7,5},{8,10},{9,11},{10,... | collective-permute-start | bytes 98312 | tf_op jit(solution)/shard_map/ppermute | solution.py:26
  4.6 0.7 %copy.21 = s32[1,1,1,3,40]{4,3,2,1,0:T(4,128)S(1)} copy(s32[1,1,1,3,40]{4,2,3,1,0:T(1,128)} %param.9) | data formatting | bytes 960
  5.3 0.7 %copy.20 = s32[1,1,1,3,40]{4,3,2,1,0:T(4,128)S(1)} copy(s32[1,1,1,3,40]{4,2,3,1,0:T(1,128)} %param.10) | data formatting | bytes 960
  6.0 0.7 %collective-permute-done.refs_5_ = bf16[128,128]{1,0:T(8,128)(2,1)S(1)} collective-permute-done((bf16[128,128]{1,0:T(8,128)(2,1)S(1)}, bf16[128,128]{1,0:T(8,128)(2,1)S(1)}, u32[]{:S(2)}, u32[]{:S(2)}) %collective-permute-start) | collective-permute-done | bytes 32800 | tf_op jit(solution)/shard_map/ppermute | solution.py:26
  6.7 2.1 %copy-done = bf16[1,1,1,3,40,128,128]{6,5,4,3,2,1,0:T(8,128)(2,1)S(1)} copy-done((bf16[1,1,1,3,40,128,128]{6,5,4,3,2,1,0:T(8,128)(2,1)S(1)}, bf16[1,1,1,3,40,128,128]{6,5,4,3,2,1,0:T(8,128)(2,1)}, u32[]{:S(2)}) %copy-start) | copy-done | bytes 3932184
  8.8 0.7 copy-done.2
  9.4 1.9 %shard_map.95 = (bf16[8,128,128]{2,1,0:T(8,128)(2,1)}, f32[16,128,128]{2,1,0:T(8,128)S(1)}) custom-call(s32[3,40]{1,0:T(4,128)S(1)} %bitcast.81, s32[3,40]{1,0:T(4,128)S(1)} %bitcast.85, s32[3]{0:T(128)S(1)} %bitcast.89, bf16[3,40,128,128]{3,2,1,0:T(8,128)(2,1)S(1)} %bitcast.69, bf16[128,128]{1,0:T(8,128)(2,1)S(1)} %convolution_convert_fusion.3.refs_4_, ...), custom_call_target="tpu_custom_call" | custom-call | tf_op jit(solution)/shard_map/pallas_call | solution.py:132
  11.4 6.4 %all-to-all-start = ((bf16[8,128,128]{2,1,0:T(8,128)(2,1)}), bf16[8,128,128]{2,1,0:T(8,128)(2,1)S(1)}, u32[]{:S(2)}, u32[]{:S(2)}) async-start(bf16[8,128,128]{2,1,0:T(8,128)(2,1)} %get-tuple-element.6), calls=%async_computation | async-start | bytes 524288 | tf_op jit(solution)/shard_map/all_to_all | solution.py:155
  18.4 1.7 %collective-permute-start.9 = (bf16[128,128]{1,0:T(8,128)(2,1)S(1)}, bf16[128,128]{1,0:T(8,128)(2,1)S(1)}, u32[]{:S(2)}, u32[]{:S(2)}) collective-permute-start(bf16[128,128]{1,0:T(8,128)(2,1)S(1)} %convolution_convert_fusion.3.refs_4_), channel_id=1, source_target_pairs={{0,3},{1,2},{2,1},{3,0},{4,7},{5,6},{6,5},{7,4},{8,11},{9,10},{10,... | collective-permute-start | bytes 98312 | tf_op jit(solution)/shard_map/ppermute | solution.py:26
  20.2 6.2 %all-to-all-done = bf16[8,128,128]{2,1,0:T(8,128)(2,1)S(1)} async-done(((bf16[8,128,128]{2,1,0:T(8,128)(2,1)}), bf16[8,128,128]{2,1,0:T(8,128)(2,1)S(1)}, u32[]{:S(2)}, u32[]{:S(2)}) %all-to-all-start) | async-done | bytes 262176 | tf_op jit(solution)/shard_map/all_to_all | solution.py:155
  26.7 1.4 %collective-permute-start.7 = (bf16[128,128]{1,0:T(8,128)(2,1)S(1)}, bf16[128,128]{1,0:T(8,128)(2,1)S(1)}, u32[]{:S(2)}, u32[]{:S(2)}) collective-permute-start(bf16[128,128]{1,0:T(8,128)(2,1)S(1)} %bitcast.73), channel_id=1, source_target_pairs={{0,3},{1,2},{2,1},{3,0},{4,7},{5,6},{6,5},{7,4},{8,11},{9,10},{10,... | collective-permute-start | bytes 98312 | tf_op jit(solution)/shard_map/ppermute | solution.py:26
  28.2 0.7 %collective-permute-start.5 = (bf16[128,128]{1,0:T(8,128)(2,1)S(1)}, bf16[128,128]{1,0:T(8,128)(2,1)S(1)}, u32[]{:S(2)}, u32[]{:S(2)}) collective-permute-start(bf16[128,128]{1,0:T(8,128)(2,1)S(1)} %bitcast.75), channel_id=1, source_target_pairs={{0,2},{1,3},{2,0},{3,1},{4,6},{5,7},{6,4},{7,5},{8,10},{9,11},{10,... | collective-permute-start | bytes 98312 | tf_op jit(solution)/shard_map/ppermute | solution.py:26
  28.9 2.4 %shard_map.96.refs_12_ = f32[16,128,128]{2,1,0:T(8,128)S(1)} custom-call(s32[3,40]{1,0:T(4,128)S(1)} %collective-permute-done.1.refs_0_.refs_4_, s32[3,40]{1,0:T(4,128)S(1)} %collective-permute-done.2.refs_1_.refs_5_, s32[3]{0:T(128)S(1)} %collective-permute-done.3.refs_2_.refs_6_, bf16[3,40,128,128]{3,2,1,0:T(8,128)(2,1)} %collective-permute-done.4.refs_3_.refs_7_, ...), custom_call_target="tpu_custom_call" | custom-call | tf_op jit(solution)/shard_map/pallas_call | solution.py:132
  31.4 0.7 %collective-permute-done.5.refs_9_ = bf16[128,128]{1,0:T(8,128)(2,1)S(1)} collective-permute-done((bf16[128,128]{1,0:T(8,128)(2,1)S(1)}, bf16[128,128]{1,0:T(8,128)(2,1)S(1)}, u32[]{:S(2)}, u32[]{:S(2)}) %collective-permute-start.5) | collective-permute-done | bytes 32800 | tf_op jit(solution)/shard_map/ppermute | solution.py:26
  32.1 2.6 %shard_map.97 = (bf16[8,128,128]{2,1,0:T(8,128)(2,1)S(1)}, f32[8,128,128]{2,1,0:T(8,128)S(1)}) custom-call(s32[3,40]{1,0:T(4,128)S(1)} %bitcast.83, s32[3,40]{1,0:T(4,128)S(1)} %bitcast.87, s32[3]{0:T(128)S(1)} %bitcast.91, bf16[3,40,128,128]{3,2,1,0:T(8,128)(2,1)S(1)} %bitcast.70, s32[3,40]{1,0:T(4,128)S(1)} %collective-permute-done.1.refs_0_.refs_4_, ...), custom_call_target="tpu_custom_call" | custom-call | tf_op jit(solution)/shard_map/pallas_call | solution.py:132
  34.7 13.6 %all_to_all.15 = bf16[8,128,128]{2,1,0:T(8,128)(2,1)S(1)} all-to-all(bf16[8,128,128]{2,1,0:T(8,128)(2,1)S(1)} %get-tuple-element.8), channel_id=1, replica_groups=mesh['prow'=8,'pcol'=2,'zgrid'=2] {'prow'}, dimensions={0} | all-to-all | bytes 524288 | tf_op jit(solution)/shard_map/all_to_all | solution.py:155
  48.5 3.9 %collective-permute-done.10.refs_9_ = bf16[128,128]{1,0:T(8,128)(2,1)S(1)} collective-permute-done((bf16[128,128]{1,0:T(8,128)(2,1)S(1)}, bf16[128,128]{1,0:T(8,128)(2,1)S(1)}, u32[]{:S(2)}, u32[]{:S(2)}) %collective-permute-start.10) | collective-permute-done | bytes 32800 | tf_op jit(solution)/shard_map/ppermute | solution.py:26
  52.4 3.3 %shard_map.98 = bf16[8,128,128]{2,1,0:T(8,128)(2,1)} custom-call(s32[3,40]{1,0:T(4,128)S(1)} %bitcast.84, s32[3,40]{1,0:T(4,128)S(1)} %bitcast.88, s32[3]{0:T(128)S(1)} %bitcast.92, bf16[3,40,128,128]{3,2,1,0:T(8,128)(2,1)S(1)} %bitcast.71, s32[3,40]{1,0:T(4,128)S(1)} %collective-permute-done.1.refs_0_.refs_4_, ...), custom_call_target="tpu_custom_call" | custom-call | tf_op jit(solution)/shard_map/pallas_call | solution.py:132
  55.7 3.4 %all-to-all-start.2 = ((bf16[8,128,128]{2,1,0:T(8,128)(2,1)}), bf16[8,128,128]{2,1,0:T(8,128)(2,1)S(1)}, u32[]{:S(2)}, u32[]{:S(2)}) async-start(bf16[8,128,128]{2,1,0:T(8,128)(2,1)} %shard_map.98), calls=%async_computation.2 | async-start | bytes 524288 | tf_op jit(solution)/shard_map/all_to_all | solution.py:155
  59.1 0.6 maximum_bitcast_fusion
  59.7 7.5 %all-to-all-done.2 = bf16[8,128,128]{2,1,0:T(8,128)(2,1)S(1)} async-done(((bf16[8,128,128]{2,1,0:T(8,128)(2,1)}), bf16[8,128,128]{2,1,0:T(8,128)(2,1)S(1)}, u32[]{:S(2)}, u32[]{:S(2)}) %all-to-all-start.2) | async-done | bytes 262176 | tf_op jit(solution)/shard_map/all_to_all | solution.py:155
  67.4 0.6 maximum_bitcast_fusion.1
  (34 shorter events, 1.4 us)
Async XLA Ops:
  0.6 25.8 %copy-start.4 = (bf16[1,1,1,2,128,128]{5,4,3,2,1,0:T(8,128)(2,1)S(1)}, bf16[1,1,1,2,128,128]{5,4,3,2,1,0:T(8,128)(2,1)}, u32[]{:S(2)}) copy-start(bf16[1,1,1,2,128,128]{5,4,3,2,1,0:T(8,128)(2,1)} %param.12) | copy-start | bytes 196612
  0.6 17.1 %copy-start.3 = (s32[1,1,1,3]{3,2,1,0:T(1,128)S(1)}, s32[1,1,1,3]{3,2,1,0:T(1,128)}, u32[]{:S(2)}) copy-start(s32[1,1,1,3]{3,2,1,0:T(1,128)} %param.11) | copy-start | bytes 40
  0.7 28.2 %collective-permute-start.4 = (bf16[3,40,128,128]{3,2,1,0:T(8,128)(2,1)}, bf16[3,40,128,128]{3,2,1,0:T(8,128)(2,1)}, u32[]{:S(2)}, u32[]{:S(2)}) collective-permute-start(bf16[3,40,128,128]{3,2,1,0:T(8,128)(2,1)} %bitcast.68), channel_id=1, source_target_pairs={{0,1},{1,0},{2,3},{3,2},{4,5},{5,4},{6,7},{7,6},{8,9},{9,8},{10,11... | collective-permute-start | bytes 11796488 | tf_op jit(solution)/shard_map/ppermute | solution.py:32
  2.1 4.6 %collective-permute-start = (bf16[128,128]{1,0:T(8,128)(2,1)S(1)}, bf16[128,128]{1,0:T(8,128)(2,1)S(1)}, u32[]{:S(2)}, u32[]{:S(2)}) collective-permute-start(bf16[128,128]{1,0:T(8,128)(2,1)S(1)} %convolution_convert_fusion.3.refs_4_), channel_id=1, source_target_pairs={{0,2},{1,3},{2,0},{3,1},{4,6},{5,7},{6,4},{7,5},{8,10},{9,11},{10,... | collective-permute-start | bytes 98312 | tf_op jit(solution)/shard_map/ppermute | solution.py:26
  6.7 2.1 %copy-start = (bf16[1,1,1,3,40,128,128]{6,5,4,3,2,1,0:T(8,128)(2,1)S(1)}, bf16[1,1,1,3,40,128,128]{6,5,4,3,2,1,0:T(8,128)(2,1)}, u32[]{:S(2)}) copy-start(bf16[1,1,1,3,40,128,128]{6,5,4,3,2,1,0:T(8,128)(2,1)} %param.8) | copy-start | bytes 11796484
  8.8 0.7 copy-start.2
  9.4 17.0 %copy-start.5 = (bf16[1,1,1,2,128,128]{5,4,3,2,1,0:T(8,128)(2,1)S(1)}, bf16[1,1,1,2,128,128]{5,4,3,2,1,0:T(8,128)(2,1)}, u32[]{:S(2)}) copy-start(bf16[1,1,1,2,128,128]{5,4,3,2,1,0:T(8,128)(2,1)} %param.14) | copy-start | bytes 196612
  11.4 15.0 %all-to-all-start = ((bf16[8,128,128]{2,1,0:T(8,128)(2,1)}), bf16[8,128,128]{2,1,0:T(8,128)(2,1)S(1)}, u32[]{:S(2)}, u32[]{:S(2)}) async-start(bf16[8,128,128]{2,1,0:T(8,128)(2,1)} %get-tuple-element.6), calls=%async_computation | async-start | bytes 524288 | tf_op jit(solution)/shard_map/all_to_all | solution.py:155
  17.8 8.8 %collective-permute-start.3 = (s32[3]{0:T(128)S(1)}, s32[3]{0:T(128)S(1)}, u32[]{:S(2)}, u32[]{:S(2)}) collective-permute-start(s32[3]{0:T(128)S(1)} %bitcast.90), channel_id=1, source_target_pairs={{0,1},{1,0},{2,3},{3,2},{4,5},{5,4},{6,7},{7,6},{8,9},{9,8},{10,11... | collective-permute-start | bytes 44 | tf_op jit(solution)/shard_map/ppermute | solution.py:32
  17.9 8.8 %collective-permute-start.2 = (s32[3,40]{1,0:T(4,128)S(1)}, s32[3,40]{1,0:T(4,128)S(1)}, u32[]{:S(2)}, u32[]{:S(2)}) collective-permute-start(s32[3,40]{1,0:T(4,128)S(1)} %bitcast.86), channel_id=1, source_target_pairs={{0,1},{1,0},{2,3},{3,2},{4,5},{5,4},{6,7},{7,6},{8,9},{9,8},{10,11... | collective-permute-start | bytes 1448 | tf_op jit(solution)/shard_map/ppermute | solution.py:32
  18.4 9.7 %collective-permute-start.1 = (s32[3,40]{1,0:T(4,128)S(1)}, s32[3,40]{1,0:T(4,128)S(1)}, u32[]{:S(2)}, u32[]{:S(2)}) collective-permute-start(s32[3,40]{1,0:T(4,128)S(1)} %bitcast.82), channel_id=1, source_target_pairs={{0,1},{1,0},{2,3},{3,2},{4,5},{5,4},{6,7},{7,6},{8,9},{9,8},{10,11... | collective-permute-start | bytes 1448 | tf_op jit(solution)/shard_map/ppermute | solution.py:32
  18.4 9.7 %collective-permute-start.9 = (bf16[128,128]{1,0:T(8,128)(2,1)S(1)}, bf16[128,128]{1,0:T(8,128)(2,1)S(1)}, u32[]{:S(2)}, u32[]{:S(2)}) collective-permute-start(bf16[128,128]{1,0:T(8,128)(2,1)S(1)} %convolution_convert_fusion.3.refs_4_), channel_id=1, source_target_pairs={{0,3},{1,2},{2,1},{3,0},{4,7},{5,6},{6,5},{7,4},{8,11},{9,10},{10,... | collective-permute-start | bytes 98312 | tf_op jit(solution)/shard_map/ppermute | solution.py:26
  26.4 5.7 %copy-start.1 = (bf16[1,1,1,3,40,128,128]{6,5,4,3,2,1,0:T(8,128)(2,1)S(1)}, bf16[1,1,1,3,40,128,128]{6,5,4,3,2,1,0:T(8,128)(2,1)}, u32[]{:S(2)}) copy-start(bf16[1,1,1,3,40,128,128]{6,5,4,3,2,1,0:T(8,128)(2,1)} %param.8) | copy-start | bytes 11796484
  26.6 2.3 %collective-permute-start.8 = (bf16[128,128]{1,0:T(8,128)(2,1)S(1)}, bf16[128,128]{1,0:T(8,128)(2,1)S(1)}, u32[]{:S(2)}, u32[]{:S(2)}) collective-permute-start(bf16[128,128]{1,0:T(8,128)(2,1)S(1)} %convolution_convert_fusion.3.refs_4_), channel_id=1, source_target_pairs={{0,1},{1,0},{2,3},{3,2},{4,5},{5,4},{6,7},{7,6},{8,9},{9,8},{10,11... | collective-permute-start | bytes 98312 | tf_op jit(solution)/shard_map/ppermute | solution.py:26
  26.7 4.7 %collective-permute-start.7 = (bf16[128,128]{1,0:T(8,128)(2,1)S(1)}, bf16[128,128]{1,0:T(8,128)(2,1)S(1)}, u32[]{:S(2)}, u32[]{:S(2)}) collective-permute-start(bf16[128,128]{1,0:T(8,128)(2,1)S(1)} %bitcast.73), channel_id=1, source_target_pairs={{0,3},{1,2},{2,1},{3,0},{4,7},{5,6},{6,5},{7,4},{8,11},{9,10},{10,... | collective-permute-start | bytes 98312 | tf_op jit(solution)/shard_map/ppermute | solution.py:26
  28.1 3.3 %collective-permute-start.6 = (bf16[128,128]{1,0:T(8,128)(2,1)S(1)}, bf16[128,128]{1,0:T(8,128)(2,1)S(1)}, u32[]{:S(2)}, u32[]{:S(2)}) collective-permute-start(bf16[128,128]{1,0:T(8,128)(2,1)S(1)} %bitcast.74), channel_id=1, source_target_pairs={{0,1},{1,0},{2,3},{3,2},{4,5},{5,4},{6,7},{7,6},{8,9},{9,8},{10,11... | collective-permute-start | bytes 98312 | tf_op jit(solution)/shard_map/ppermute | solution.py:26
  28.2 3.9 %collective-permute-start.5 = (bf16[128,128]{1,0:T(8,128)(2,1)S(1)}, bf16[128,128]{1,0:T(8,128)(2,1)S(1)}, u32[]{:S(2)}, u32[]{:S(2)}) collective-permute-start(bf16[128,128]{1,0:T(8,128)(2,1)S(1)} %bitcast.75), channel_id=1, source_target_pairs={{0,2},{1,3},{2,0},{3,1},{4,6},{5,7},{6,4},{7,5},{8,10},{9,11},{10,... | collective-permute-start | bytes 98312 | tf_op jit(solution)/shard_map/ppermute | solution.py:26
  31.3 17.0 %copy-start.6 = (bf16[1,1,2,128,128]{4,3,2,1,0:T(8,128)(2,1)S(1)}, bf16[1,1,2,128,128]{4,3,2,1,0:T(8,128)(2,1)}, u32[]{:S(2)}) copy-start(bf16[1,1,2,128,128]{4,3,2,1,0:T(8,128)(2,1)} %param.15) | copy-start | bytes 196612
  31.3 17.0 %copy-start.7 = (bf16[1,1,2,128,128]{4,3,2,1,0:T(8,128)(2,1)S(1)}, bf16[1,1,2,128,128]{4,3,2,1,0:T(8,128)(2,1)}, u32[]{:S(2)}) copy-start(bf16[1,1,2,128,128]{4,3,2,1,0:T(8,128)(2,1)} %param.13) | copy-start | bytes 196612
  48.5 3.9 %collective-permute-start.10 = (bf16[128,128]{1,0:T(8,128)(2,1)S(1)}, bf16[128,128]{1,0:T(8,128)(2,1)S(1)}, u32[]{:S(2)}, u32[]{:S(2)}) collective-permute-start(bf16[128,128]{1,0:T(8,128)(2,1)S(1)} %bitcast.78), channel_id=1, source_target_pairs={{0,2},{1,3},{2,0},{3,1},{4,6},{5,7},{6,4},{7,5},{8,10},{9,11},{10,... | collective-permute-start | bytes 98312 | tf_op jit(solution)/shard_map/ppermute | solution.py:26
  55.7 11.6 %all-to-all-start.2 = ((bf16[8,128,128]{2,1,0:T(8,128)(2,1)}), bf16[8,128,128]{2,1,0:T(8,128)(2,1)S(1)}, u32[]{:S(2)}, u32[]{:S(2)}) async-start(bf16[8,128,128]{2,1,0:T(8,128)(2,1)} %shard_map.98), calls=%async_computation.2 | async-start | bytes 524288 | tf_op jit(solution)/shard_map/all_to_all | solution.py:155

commit v3 on v2

v3 whole, which is shorter than its diff:
```python
import functools

import jax
import jax.numpy as jnp
from jax import lax
from jax.experimental import pallas as pl
from jax.experimental.pallas import tpu as pltpu
from jax.sharding import PartitionSpec as P

slot_group = 8
code_shift = 8


def partner(index, k, size):
    if size & (size - 1) == 0:
        return index ^ k
    return lax.rem(index + k, size) if not isinstance(index, int) else (index + k) % size


def origin(index, k, size):
    if size & (size - 1) == 0:
        return index ^ k
    return (index - k) % size


def sibling_values(value, layers):
    cols = lax.axis_size("pcol")
    depth = lax.axis_size("zgrid")
    found = []
    for k in range(cols):
        if k == 0 and layers == 0:
            found.append(value)
            continue
        moves = []
        for c in range(cols):
            for z in range(depth):
                target = ((c - k) % cols) * depth + (z - layers) % depth
                moves.append((c * depth + z, target))
        found.append(lax.ppermute(value, ("pcol", "zgrid"), moves))
    return found


def from_other_core(value, shift):
    depth = lax.axis_size("zgrid")
    return lax.ppermute(value, "zgrid", [(z, (z - shift) % depth) for z in range(depth)])


def update_kernel(config, *refs):
    sets, cols, row_count, lowest_kept, layer_count, carries, sends, keeps, staged = config
    refs = list(refs)
    solution_sets = 1 + max(s[2] for s in sets)
    codes = [refs.pop(0) for _ in range(layer_count)]
    blocks = [refs.pop(0) for _ in range(layer_count)]
    solutions = [refs.pop(0) for _ in range(solution_sets * cols)]
    total_in = refs.pop(0) if carries else None
    send_refs = [refs.pop(0) for _ in range(row_count)] if sends else []
    kept_ref = refs.pop(0) if keeps else None
    chosen, total = refs[:2]
    capacity = blocks[0].shape[1]
    groups = capacity // slot_group

    if staged:
        buffer, semaphores = refs[2:]

        def group_copy(k, g):
            part = pl.ds(g * slot_group, slot_group)
            return pltpu.make_async_copy(
                blocks[sets[k][3]].at[sets[k][0], part], buffer.at[k, part], semaphores.at[k, g]
            )

        for k in range(len(sets)):
            for g in range(groups):
                group_copy(k, g).start()

    if carries:
        total[: total_in.shape[0]] = total_in[...]
    else:
        total[...] = jnp.zeros_like(total)
    spare = total.shape[0] - 1
    for j in range(solution_sets * cols):
        chosen[j] = solutions[j][...]

    for k in range(len(sets)):
        level, lowest, solution_index, layer_index = sets[k]
        code = codes[layer_index]

        def one_group(g, unused):
            first = g * slot_group
            if staged:
                group_copy(k, g).wait()
            for s in range(slot_group):
                slot = first + s
                value = code[level, 0, slot]
                aim = lax.shift_right_logical(value, code_shift)
                place = jnp.where(aim < lowest * row_count, spare, aim - lowest_kept * row_count)
                column = solution_index * cols + (value & ((1 << code_shift) - 1))
                piece = buffer[k, slot] if staged else blocks[layer_index][level, slot]
                total[place] += jnp.dot(
                    piece, chosen[column], preferred_element_type=jnp.float32
                )
            return unused

        lax.fori_loop(0, groups, one_group, 0)

    if sends:
        me = lax.axis_index("prow")
        for k in range(row_count):
            send_refs[k][...] = total[partner(me, k, row_count)].astype(jnp.bfloat16)
    if keeps:
        first = row_count if sends else 0
        kept_ref[...] = total[first:spare]


def update(sets, layers, solution_groups, total_in, row_count, lowest_kept, sends, keeps, staged):
    cols = len(solution_groups[0])
    width, sides = solution_groups[0][0].shape
    capacity = layers[0][1].shape[1]
    sections = 3 - lowest_kept
    solutions = [part for group in solution_groups for part in group]
    operands = [a[0] for a in layers] + [a[1] for a in layers] + solutions
    block_space = pltpu.HBM if staged else pltpu.VMEM
    specs = [pl.BlockSpec(memory_space=pltpu.SMEM)] * len(layers)
    specs += [pl.BlockSpec(memory_space=block_space)] * len(layers)
    specs += [pl.BlockSpec(memory_space=pltpu.VMEM)] * len(solutions)
    if total_in is not None:
        operands.append(total_in)
        specs.append(pl.BlockSpec(memory_space=pltpu.VMEM))
    outs = []
    if sends:
        outs += [jax.ShapeDtypeStruct((width, sides), jnp.bfloat16)] * row_count
    if keeps:
        kept = (sections - int(sends)) * row_count
        outs.append(jax.ShapeDtypeStruct((kept, width, sides), jnp.float32))
    scratch = [
        pltpu.VMEM((len(solutions), width, sides), jnp.bfloat16),
        pltpu.VMEM((sections * row_count + 1, width, sides), jnp.float32),
    ]
    if staged:
        scratch += [
            pltpu.VMEM((len(sets), capacity, width, width), jnp.bfloat16),
            pltpu.SemaphoreType.DMA((len(sets), capacity // slot_group)),
        ]
    config = (
        sets, cols, row_count, lowest_kept, len(layers), total_in is not None, sends, keeps, staged,
    )
    found = pl.pallas_call(
        functools.partial(update_kernel, config),
        out_shape=outs,
        in_specs=specs,
        out_specs=[pl.BlockSpec(memory_space=pltpu.VMEM)] * len(outs),
        scratch_shapes=scratch,
        compiler_params=pltpu.CompilerParams(vmem_limit_bytes=48 * 1024 * 1024),
    )(*operands)
    return list(found[:row_count]) if sends else [], found[-1] if keeps else None


def exchange(parts):
    size = len(parts)
    found = [parts[0]]
    for k in range(1, size):
        moves = [(j, partner(j, k, size)) for j in range(size)]
        found.append(lax.ppermute(parts[k], "prow", moves))
    return found


def solve_block(inverse, residual):
    return jnp.dot(inverse, residual, preferred_element_type=jnp.float32).astype(jnp.bfloat16)


def solve_from(received, given, inverse):
    terms = [part.astype(jnp.float32) for part in received]
    while len(terms) > 1:
        terms = [sum(terms[i : i + 2]) for i in range(0, len(terms), 2)]
    residual = (given.astype(jnp.float32) - terms[0]).astype(jnp.bfloat16)
    return solve_block(inverse, residual)


def local(blocks, sources, targets, counts, given_sub, given_top, inverse_sub, inverse_top):
    row_count = lax.axis_size("prow")
    cols = lax.axis_size("pcol")
    depth = lax.axis_size("zgrid")
    levels, capacity = sources.shape[3:]
    block_set = blocks[0, 0, 0]
    right_sub = given_sub[0, 0, 0]
    right_top = given_top[0, 0]
    factor_sub = inverse_sub[0, 0, 0]
    factor_top = inverse_top[0, 0]

    alive = jnp.arange(capacity)[None, None, :] < counts.reshape(levels, 1, 1)
    column = (sources.reshape(levels, 1, capacity) - lax.axis_index("pcol")) % cols
    aim = jnp.where(alive, targets.reshape(levels, 1, capacity), levels * row_count)
    code = (aim << code_shift) + column

    others = [
        (from_other_core(code, m), from_other_core(block_set, m)) for m in range(1, depth)
    ]
    both = [(code, block_set)] + others

    level_zero = solve_block(factor_sub[0], right_sub[0])
    spread_zero = [sibling_values(level_zero, m) for m in range(depth)]
    sends, total = update(
        [(0, 0, 0, 0)], both[:1], spread_zero[:1], None, row_count, 0, True, True, True
    )
    sends, spread_rest = lax.optimization_barrier((sends, spread_zero[1:]))
    received = exchange(sends)
    _, total = update(
        [(0, 1, m, m) for m in range(depth - 1)],
        others, spread_rest, total, row_count, 1, False, True, False,
    )
    received, total = lax.optimization_barrier((received, total))
    level_one = solve_from(received, right_sub[1], factor_sub[1])
    spread_one = [sibling_values(level_one, m) for m in range(depth)]
    sends, total = update(
        [(1, 1, m, m) for m in range(depth)],
        both, spread_one, total, row_count, 1, True, True, False,
    )
    level_two = solve_from(exchange(sends), right_top[0], factor_top[0])
    spread_two = sibling_values(level_two, 0)
    sends, _ = update(
        [(2, 2, 0, m) for m in range(depth)],
        both, [spread_two], total, row_count, 2, True, False, False,
    )
    level_three = solve_from(exchange(sends), right_top[1], factor_top[1])
    solved_sub = jnp.stack([level_zero, level_one])[None, None, None]
    solved_top = jnp.stack([level_two, level_three])[None, None]
    return (solved_sub, solved_top)


def solution(mesh):
    in_specs = (
        P("prow", "pcol", "zgrid", None, None, None, None),
        P("prow", "pcol", "zgrid", None, None),
        P("prow", "pcol", "zgrid", None, None),
        P("prow", "pcol", "zgrid", None),
        P("prow", "pcol", "zgrid", None, None, None),
        P("prow", "pcol", None, None, None),
        P("prow", "pcol", "zgrid", None, None, None),
        P("prow", "pcol", None, None, None),
    )
    out_specs = (P("prow", "pcol", "zgrid", None, None, None), P("prow", "pcol", None, None, None))
    return jax.shard_map(local, mesh=mesh, in_specs=in_specs, out_specs=out_specs, check_vma=False)
```

time: 69.4 us -> 80.8 us (1.16); the launches traced: 68.1 us -> 80.5 us
  starting transfers between devices: 17.6 us -> 40.8 us
  blocking collectives: 13.6 us -> 0 us
  Pallas kernels: 10.2 us -> 14.7 us
  local copies, waits for them, and re-layouts: 4.16 us -> 2.14 us
    ppermute x7 -> x28, starting transfers between devices: 6.57 us -> 40.3 us  [the longest x21 33.6 us: exchange(): found.append(lax.ppermute(parts[k], 'prow', moves))]
    all_to_all x2 -> x0, waiting for transfers between devices: 13.7 us -> none  [reduced_solve(): received = lax.all_to_all(send, 'prow', 0, 0, tiled=True)]
    all_to_all x1 -> x0, blocking collectives: 13.6 us -> none  [reduced_solve(): received = lax.all_to_all(send, 'prow', 0, 0, tiled=True)]
    ppermute x7 -> x28, waiting for transfers between devices: 5.31 us -> 17.9 us  [the longest x21 10.1 us: exchange(): found.append(lax.ppermute(parts[k], 'prow', moves))]
    all_to_all x2 -> x0, starting transfers between devices: 9.83 us -> none  [reduced_solve(): received = lax.all_to_all(send, 'prow', 0, 0, tiled=True)]
    pallas_call x4, Pallas kernels: 10.2 us -> 14.7 us  [update(): pl.pallas_call(functools.partial(update_kernel, config), out_shape=outs,...]
    unnamed x18 -> x12, local copies, waits for them, and re-layouts: 4.16 us -> 2.14 us
  transfers between devices with their start and end apart: 13 -> 30, of which waited for: 5 -> 10; matrix products, arithmetic and copies ran while one was open for 5% -> 3% of each run, Pallas kernels for 6% -> 7%
where the time goes in v3:
time: 80.8 us; the launch traced here: 80.5 us
  starting transfers between devices  40.8 us (50%)
  waiting for transfers between devices  18.7 us (23%)
  Pallas kernels  14.7 us (18%)
  local copies, waits for them, and re-layouts  2.14 us (3%)
  other arithmetic  2.05 us (3%)
  matrix products  1.38 us (2%)
    ppermute x21, starting transfers between devices, exchange(): found.append(lax.ppermute(parts[k], 'prow', moves))  33.6 us
    pallas_call x4, Pallas kernels, update(): pl.pallas_call(functools.partial(update_kernel, config), out_shape=outs,...  14.7 us
    ppermute x21, waiting for transfers between devices, exchange(): found.append(lax.ppermute(parts[k], 'prow', moves))  10.1 us
    ppermute x7, waiting for transfers between devices, sibling_values(): found.append(lax.ppermute(value, ('pcol', 'zgrid'), moves))  7.84 us
    ppermute x7, starting transfers between devices, sibling_values(): found.append(lax.ppermute(value, ('pcol', 'zgrid'), moves))  6.67 us
    unnamed x12, local copies, waits for them, and re-layouts  2.14 us
  transfers between devices with their start and end apart: 30, of which 10 were waited for; matrix products, arithmetic and copies ran while one was open for 3% of the time, Pallas kernels for 7%

profile of v3, /device:TPU:0, one launch (start us, length us, event | category | flops | bytes accessed | tf_op | source)
XLA Modules:
  0.0 80.5 jit_solution(9636761350788885045)
XLA Ops:
  2.0 2.6 %collective-permute-start.2 = (bf16[128,128]{1,0:T(8,128)(2,1)S(1)}, bf16[128,128]{1,0:T(8,128)(2,1)S(1)}, u32[]{:S(2)}, u32[]{:S(2)}) collective-permute-start(bf16[128,128]{1,0:T(8,128)(2,1)S(1)} %convolution_convert_fusion.3.refs_2_), channel_id=1, source_target_pairs={{0,3},{1,2},{2,1},{3,0},{4,7},{5,6},{6,5},{7,4},{8,11},{9,10},{10,... | collective-permute-start | bytes 98312 | tf_op jit(solution)/shard_map/ppermute | solution.py:39
  5.9 2.7 %collective-permute-done.refs_3_ = bf16[128,128]{1,0:T(8,128)(2,1)S(1)} collective-permute-done((bf16[128,128]{1,0:T(8,128)(2,1)S(1)}, bf16[128,128]{1,0:T(8,128)(2,1)S(1)}, u32[]{:S(2)}, u32[]{:S(2)}) %collective-permute-start) | collective-permute-done | bytes 32800 | tf_op jit(solution)/shard_map/ppermute | solution.py:39
  8.6 2.1 %copy-done = bf16[1,1,1,3,40,128,128]{6,5,4,3,2,1,0:T(8,128)(2,1)S(1)} copy-done((bf16[1,1,1,3,40,128,128]{6,5,4,3,2,1,0:T(8,128)(2,1)S(1)}, bf16[1,1,1,3,40,128,128]{6,5,4,3,2,1,0:T(8,128)(2,1)}, u32[]{:S(2)}) %copy-start) | copy-done | bytes 3932184
  10.7 2.1 %shard_map.95 = (bf16[128,128]{1,0:T(8,128)(2,1)S(1)}, bf16[128,128]{1,0:T(8,128)(2,1)S(1)}, bf16[128,128]{1,0:T(8,128)(2,1)S(1)}, bf16[128,128]{1,0:T(8,128)(2,...) custom-call(s32[3,1,40]{2,1,0:T(1,128)S(1)} %fusion.23.refs_0_, ...), custom_call_target="tpu_custom_call" | custom-call | tf_op jit(solution)/shard_map/pallas_call | solution.py:146
  12.9 1.6 %collective-permute-start.3 = (bf16[128,128]{1,0:T(8,128)(2,1)S(1)}, bf16[128,128]{1,0:T(8,128)(2,1)S(1)}, u32[]{:S(2)}, u32[]{:S(2)}) collective-permute-start(bf16[128,128]{1,0:T(8,128)(2,1)S(1)} %get-tuple-element.56), channel_id=1, source_target_pairs={{0,4},{4,0},{8,12},{12,8},{16,20},{20,16},{24,28},{28,24},{1,5},{5... | collective-permute-start | bytes 98312 | tf_op jit(solution)/shard_map/ppermute | solution.py:162
  14.4 1.6 %collective-permute-start.4 = (bf16[128,128]{1,0:T(8,128)(2,1)S(1)}, bf16[128,128]{1,0:T(8,128)(2,1)S(1)}, u32[]{:S(2)}, u32[]{:S(2)}) collective-permute-start(bf16[128,128]{1,0:T(8,128)(2,1)S(1)} %get-tuple-element.57), channel_id=1, source_target_pairs={{0,8},{4,12},{8,0},{12,4},{16,24},{20,28},{24,16},{28,20},{1,9},{5... | collective-permute-start | bytes 98312 | tf_op jit(solution)/shard_map/ppermute | solution.py:162
  17.2 2.6 %collective-permute-start.6 = (bf16[128,128]{1,0:T(8,128)(2,1)S(1)}, bf16[128,128]{1,0:T(8,128)(2,1)S(1)}, u32[]{:S(2)}, u32[]{:S(2)}) collective-permute-start(bf16[128,128]{1,0:T(8,128)(2,1)S(1)} %get-tuple-element.59), channel_id=1, source_target_pairs={{0,16},{4,20},{8,24},{12,28},{16,0},{20,4},{24,8},{28,12},{1,17},{... | collective-permute-start | bytes 98312 | tf_op jit(solution)/shard_map/ppermute | solution.py:162
  20.4 3.5 %collective-permute-start.8 = (bf16[128,128]{1,0:T(8,128)(2,1)S(1)}, bf16[128,128]{1,0:T(8,128)(2,1)S(1)}, u32[]{:S(2)}, u32[]{:S(2)}) collective-permute-start(bf16[128,128]{1,0:T(8,128)(2,1)S(1)} %get-tuple-element.61), channel_id=1, source_target_pairs={{0,24},{4,28},{8,16},{12,20},{16,8},{20,12},{24,0},{28,4},{1,25},{... | collective-permute-start | bytes 98312 | tf_op jit(solution)/shard_map/ppermute | solution.py:162
  24.8 3.4 %shard_map.96.refs_8_ = f32[16,128,128]{2,1,0:T(8,128)S(1)} custom-call(s32[3,1,40]{2,1,0:T(1,128)S(1)} %collective-permute-done.10.refs_0_.refs_1_, bf16[3,40,128,128]{3,2,1,0:T(8,128)(2,1)} %collective-permute-done.11.refs_1_.refs_3_, bf16[128,128]{1,0:T(8,128)(2,1)S(1)} %collective-permute-done.1.refs_2_, ...), custom_call_target="tpu_custom_call" | custom-call | tf_op jit(solution)/shard_map/pallas_call | solution.py:146
  28.3 2.2 %collective-permute-done.9 = bf16[128,128]{1,0:T(8,128)(2,1)S(1)} collective-permute-done((bf16[128,128]{1,0:T(8,128)(2,1)S(1)}, bf16[128,128]{1,0:T(8,128)(2,1)S(1)}, u32[]{:S(2)}, u32[]{:S(2)}) %collective-permute-start.9) | collective-permute-done | bytes 32800 | tf_op jit(solution)/shard_map/ppermute | solution.py:162
  34.1 1.4 %collective-permute-done.12.refs_5_ = bf16[128,128]{1,0:T(8,128)(2,1)S(1)} collective-permute-done((bf16[128,128]{1,0:T(8,128)(2,1)S(1)}, bf16[128,128]{1,0:T(8,128)(2,1)S(1)}, u32[]{:S(2)}, u32[]{:S(2)}) %collective-permute-start.12) | collective-permute-done | bytes 32800 | tf_op jit(solution)/shard_map/ppermute | solution.py:39
  35.5 4.6 %shard_map.97 = (bf16[128,128]{1,0:T(8,128)(2,1)S(1)}, bf16[128,128]{1,0:T(8,128)(2,1)S(1)}, bf16[128,128]{1,0:T(8,128)(2,1)S(1)}, bf16[128,128]{1,0:T(8,128)(2,...) custom-call(s32[3,1,40]{2,1,0:T(1,128)S(1)} %fusion.23.refs_0_, ...), custom_call_target="tpu_custom_call" | custom-call | tf_op jit(solution)/shard_map/pallas_call | solution.py:146
  40.7 2.9 %collective-permute-start.17 = (bf16[128,128]{1,0:T(8,128)(2,1)S(1)}, bf16[128,128]{1,0:T(8,128)(2,1)S(1)}, u32[]{:S(2)}, u32[]{:S(2)}) collective-permute-start(bf16[128,128]{1,0:T(8,128)(2,1)S(1)} %get-tuple-element.78), channel_id=1, source_target_pairs={{0,12},{4,8},{8,4},{12,0},{16,28},{20,24},{24,20},{28,16},{1,13},{... | collective-permute-start | bytes 98312 | tf_op jit(solution)/shard_map/ppermute | solution.py:162
  43.7 2.9 %collective-permute-start.19 = (bf16[128,128]{1,0:T(8,128)(2,1)S(1)}, bf16[128,128]{1,0:T(8,128)(2,1)S(1)}, u32[]{:S(2)}, u32[]{:S(2)}) collective-permute-start(bf16[128,128]{1,0:T(8,128)(2,1)S(1)} %get-tuple-element.80), channel_id=1, source_target_pairs={{0,20},{4,16},{8,28},{12,24},{16,4},{20,0},{24,12},{28,8},{1,21},{... | collective-permute-start | bytes 98312 | tf_op jit(solution)/shard_map/ppermute | solution.py:162
  46.6 1.7 %collective-permute-start.20 = (bf16[128,128]{1,0:T(8,128)(2,1)S(1)}, bf16[128,128]{1,0:T(8,128)(2,1)S(1)}, u32[]{:S(2)}, u32[]{:S(2)}) collective-permute-start(bf16[128,128]{1,0:T(8,128)(2,1)S(1)} %get-tuple-element.81), channel_id=1, source_target_pairs={{0,24},{4,28},{8,16},{12,20},{16,8},{20,12},{24,0},{28,4},{1,25},{... | collective-permute-start | bytes 98312 | tf_op jit(solution)/shard_map/ppermute | solution.py:162
  48.2 3.1 %collective-permute-start.21 = (bf16[128,128]{1,0:T(8,128)(2,1)S(1)}, bf16[128,128]{1,0:T(8,128)(2,1)S(1)}, u32[]{:S(2)}, u32[]{:S(2)}) collective-permute-start(bf16[128,128]{1,0:T(8,128)(2,1)S(1)} %get-tuple-element.82), channel_id=1, source_target_pairs={{0,28},{4,24},{8,20},{12,16},{16,12},{20,8},{24,4},{28,0},{1,29},{... | collective-permute-start | bytes 98312 | tf_op jit(solution)/shard_map/ppermute | solution.py:162
  52.3 2.6 %collective-permute-done.21 = bf16[128,128]{1,0:T(8,128)(2,1)S(1)} collective-permute-done((bf16[128,128]{1,0:T(8,128)(2,1)S(1)}, bf16[128,128]{1,0:T(8,128)(2,1)S(1)}, u32[]{:S(2)}, u32[]{:S(2)}) %collective-permute-start.21) | collective-permute-done | bytes 32800 | tf_op jit(solution)/shard_map/ppermute | solution.py:162
  56.4 2.6 %collective-permute-done.22.refs_5_ = bf16[128,128]{1,0:T(8,128)(2,1)S(1)} collective-permute-done((bf16[128,128]{1,0:T(8,128)(2,1)S(1)}, bf16[128,128]{1,0:T(8,128)(2,1)S(1)}, u32[]{:S(2)}, u32[]{:S(2)}) %collective-permute-start.22) | collective-permute-done | bytes 32800 | tf_op jit(solution)/shard_map/ppermute | solution.py:39
  58.9 4.5 %shard_map.98 = (bf16[128,128]{1,0:T(8,128)(2,1)S(1)}, bf16[128,128]{1,0:T(8,128)(2,1)S(1)}, bf16[128,128]{1,0:T(8,128)(2,1)S(1)}, bf16[128,128]{1,0:T(8,128)(2,...) custom-call(s32[3,1,40]{2,1,0:T(1,128)S(1)} %fusion.23.refs_0_, ...), custom_call_target="tpu_custom_call" | custom-call | tf_op jit(solution)/shard_map/pallas_call | solution.py:146
  64.1 2.9 %collective-permute-start.25 = (bf16[128,128]{1,0:T(8,128)(2,1)S(1)}, bf16[128,128]{1,0:T(8,128)(2,1)S(1)}, u32[]{:S(2)}, u32[]{:S(2)}) collective-permute-start(bf16[128,128]{1,0:T(8,128)(2,1)S(1)} %get-tuple-element.87), channel_id=1, source_target_pairs={{0,12},{4,8},{8,4},{12,0},{16,28},{20,24},{24,20},{28,16},{1,13},{... | collective-permute-start | bytes 98312 | tf_op jit(solution)/shard_map/ppermute | solution.py:162
  67.8 2.2 %collective-permute-start.27 = (bf16[128,128]{1,0:T(8,128)(2,1)S(1)}, bf16[128,128]{1,0:T(8,128)(2,1)S(1)}, u32[]{:S(2)}, u32[]{:S(2)}) collective-permute-start(bf16[128,128]{1,0:T(8,128)(2,1)S(1)} %get-tuple-element.89), channel_id=1, source_target_pairs={{0,20},{4,16},{8,28},{12,24},{16,4},{20,0},{24,12},{28,8},{1,21},{... | collective-permute-start | bytes 98312 | tf_op jit(solution)/shard_map/ppermute | solution.py:162
  69.9 3.1 %collective-permute-start.28 = (bf16[128,128]{1,0:T(8,128)(2,1)S(1)}, bf16[128,128]{1,0:T(8,128)(2,1)S(1)}, u32[]{:S(2)}, u32[]{:S(2)}) collective-permute-start(bf16[128,128]{1,0:T(8,128)(2,1)S(1)} %get-tuple-element.90), channel_id=1, source_target_pairs={{0,24},{4,28},{8,16},{12,20},{16,8},{20,12},{24,0},{28,4},{1,25},{... | collective-permute-start | bytes 98312 | tf_op jit(solution)/shard_map/ppermute | solution.py:162
  73.1 1.6 %collective-permute-start.29 = (bf16[128,128]{1,0:T(8,128)(2,1)S(1)}, bf16[128,128]{1,0:T(8,128)(2,1)S(1)}, u32[]{:S(2)}, u32[]{:S(2)}) collective-permute-start(bf16[128,128]{1,0:T(8,128)(2,1)S(1)} %get-tuple-element.91), channel_id=1, source_target_pairs={{0,28},{4,24},{8,20},{12,16},{16,12},{20,8},{24,4},{28,0},{1,29},{... | collective-permute-start | bytes 98312 | tf_op jit(solution)/shard_map/ppermute | solution.py:162
  75.8 3.9 %collective-permute-done.29 = bf16[128,128]{1,0:T(8,128)(2,1)S(1)} collective-permute-done((bf16[128,128]{1,0:T(8,128)(2,1)S(1)}, bf16[128,128]{1,0:T(8,128)(2,1)S(1)}, u32[]{:S(2)}, u32[]{:S(2)}) %collective-permute-start.29) | collective-permute-done | bytes 32800 | tf_op jit(solution)/shard_map/ppermute | solution.py:162
  (59 shorter events, 15.3 us)
Async XLA Ops:
  0.6 23.3 %collective-permute-start.11 = (bf16[3,40,128,128]{3,2,1,0:T(8,128)(2,1)}, bf16[3,40,128,128]{3,2,1,0:T(8,128)(2,1)}, u32[]{:S(2)}, u32[]{:S(2)}) collective-permute-start(bf16[3,40,128,128]{3,2,1,0:T(8,128)(2,1)} %bitcast.54), channel_id=1, source_target_pairs={{0,1},{1,0},{2,3},{3,2},{4,5},{5,4},{6,7},{7,6},{8,9},{9,8},{10,11... | collective-permute-start | bytes 11796488 | tf_op jit(solution)/shard_map/ppermute | solution.py:45
  2.0 10.8 %collective-permute-start.2 = (bf16[128,128]{1,0:T(8,128)(2,1)S(1)}, bf16[128,128]{1,0:T(8,128)(2,1)S(1)}, u32[]{:S(2)}, u32[]{:S(2)}) collective-permute-start(bf16[128,128]{1,0:T(8,128)(2,1)S(1)} %convolution_convert_fusion.3.refs_2_), channel_id=1, source_target_pairs={{0,3},{1,2},{2,1},{3,0},{4,7},{5,6},{6,5},{7,4},{8,11},{9,10},{10,... | collective-permute-start | bytes 98312 | tf_op jit(solution)/shard_map/ppermute | solution.py:39
  4.7 8.2 %collective-permute-start.1 = (bf16[128,128]{1,0:T(8,128)(2,1)S(1)}, bf16[128,128]{1,0:T(8,128)(2,1)S(1)}, u32[]{:S(2)}, u32[]{:S(2)}) collective-permute-start(bf16[128,128]{1,0:T(8,128)(2,1)S(1)} %convolution_convert_fusion.3.refs_2_), channel_id=1, source_target_pairs={{0,1},{1,0},{2,3},{3,2},{4,5},{5,4},{6,7},{7,6},{8,9},{9,8},{10,11... | collective-permute-start | bytes 98312 | tf_op jit(solution)/shard_map/ppermute | solution.py:39
  12.9 6.9 %collective-permute-start.3 = (bf16[128,128]{1,0:T(8,128)(2,1)S(1)}, bf16[128,128]{1,0:T(8,128)(2,1)S(1)}, u32[]{:S(2)}, u32[]{:S(2)}) collective-permute-start(bf16[128,128]{1,0:T(8,128)(2,1)S(1)} %get-tuple-element.56), channel_id=1, source_target_pairs={{0,4},{4,0},{8,12},{12,8},{16,20},{20,16},{24,28},{28,24},{1,5},{5... | collective-permute-start | bytes 98312 | tf_op jit(solution)/shard_map/ppermute | solution.py:162
  14.4 5.9 %collective-permute-start.4 = (bf16[128,128]{1,0:T(8,128)(2,1)S(1)}, bf16[128,128]{1,0:T(8,128)(2,1)S(1)}, u32[]{:S(2)}, u32[]{:S(2)}) collective-permute-start(bf16[128,128]{1,0:T(8,128)(2,1)S(1)} %get-tuple-element.57), channel_id=1, source_target_pairs={{0,8},{4,12},{8,0},{12,4},{16,24},{20,28},{24,16},{28,20},{1,9},{5... | collective-permute-start | bytes 98312 | tf_op jit(solution)/shard_map/ppermute | solution.py:162
  16.0 12.3 %collective-permute-start.5 = (bf16[128,128]{1,0:T(8,128)(2,1)S(1)}, bf16[128,128]{1,0:T(8,128)(2,1)S(1)}, u32[]{:S(2)}, u32[]{:S(2)}) collective-permute-start(bf16[128,128]{1,0:T(8,128)(2,1)S(1)} %get-tuple-element.58), channel_id=1, source_target_pairs={{0,12},{4,8},{8,4},{12,0},{16,28},{20,24},{24,20},{28,16},{1,13},{... | collective-permute-start | bytes 98312 | tf_op jit(solution)/shard_map/ppermute | solution.py:162
  17.2 11.1 %collective-permute-start.6 = (bf16[128,128]{1,0:T(8,128)(2,1)S(1)}, bf16[128,128]{1,0:T(8,128)(2,1)S(1)}, u32[]{:S(2)}, u32[]{:S(2)}) collective-permute-start(bf16[128,128]{1,0:T(8,128)(2,1)S(1)} %get-tuple-element.59), channel_id=1, source_target_pairs={{0,16},{4,20},{8,24},{12,28},{16,0},{20,4},{24,8},{28,12},{1,17},{... | collective-permute-start | bytes 98312 | tf_op jit(solution)/shard_map/ppermute | solution.py:162
  19.8 8.5 %collective-permute-start.7 = (bf16[128,128]{1,0:T(8,128)(2,1)S(1)}, bf16[128,128]{1,0:T(8,128)(2,1)S(1)}, u32[]{:S(2)}, u32[]{:S(2)}) collective-permute-start(bf16[128,128]{1,0:T(8,128)(2,1)S(1)} %get-tuple-element.60), channel_id=1, source_target_pairs={{0,20},{4,16},{8,28},{12,24},{16,4},{20,0},{24,12},{28,8},{1,21},{... | collective-permute-start | bytes 98312 | tf_op jit(solution)/shard_map/ppermute | solution.py:162
  20.4 7.9 %collective-permute-start.8 = (bf16[128,128]{1,0:T(8,128)(2,1)S(1)}, bf16[128,128]{1,0:T(8,128)(2,1)S(1)}, u32[]{:S(2)}, u32[]{:S(2)}) collective-permute-start(bf16[128,128]{1,0:T(8,128)(2,1)S(1)} %get-tuple-element.61), channel_id=1, source_target_pairs={{0,24},{4,28},{8,16},{12,20},{16,8},{20,12},{24,0},{28,4},{1,25},{... | collective-permute-start | bytes 98312 | tf_op jit(solution)/shard_map/ppermute | solution.py:162
  23.9 6.6 %collective-permute-start.9 = (bf16[128,128]{1,0:T(8,128)(2,1)S(1)}, bf16[128,128]{1,0:T(8,128)(2,1)S(1)}, u32[]{:S(2)}, u32[]{:S(2)}) collective-permute-start(bf16[128,128]{1,0:T(8,128)(2,1)S(1)} %get-tuple-element.62), channel_id=1, source_target_pairs={{0,28},{4,24},{8,20},{12,16},{16,12},{20,8},{24,4},{28,0},{1,29},{... | collective-permute-start | bytes 98312 | tf_op jit(solution)/shard_map/ppermute | solution.py:162
  40.1 6.5 %collective-permute-start.15 = (bf16[128,128]{1,0:T(8,128)(2,1)S(1)}, bf16[128,128]{1,0:T(8,128)(2,1)S(1)}, u32[]{:S(2)}, u32[]{:S(2)}) collective-permute-start(bf16[128,128]{1,0:T(8,128)(2,1)S(1)} %get-tuple-element.76), channel_id=1, source_target_pairs={{0,4},{4,0},{8,12},{12,8},{16,20},{20,16},{24,28},{28,24},{1,5},{5... | collective-permute-start | bytes 98312 | tf_op jit(solution)/shard_map/ppermute | solution.py:162
  40.7 7.5 %collective-permute-start.16 = (bf16[128,128]{1,0:T(8,128)(2,1)S(1)}, bf16[128,128]{1,0:T(8,128)(2,1)S(1)}, u32[]{:S(2)}, u32[]{:S(2)}) collective-permute-start(bf16[128,128]{1,0:T(8,128)(2,1)S(1)} %get-tuple-element.77), channel_id=1, source_target_pairs={{0,8},{4,12},{8,0},{12,4},{16,24},{20,28},{24,16},{28,20},{1,9},{5... | collective-permute-start | bytes 98312 | tf_op jit(solution)/shard_map/ppermute | solution.py:162
  40.7 10.6 %collective-permute-start.17 = (bf16[128,128]{1,0:T(8,128)(2,1)S(1)}, bf16[128,128]{1,0:T(8,128)(2,1)S(1)}, u32[]{:S(2)}, u32[]{:S(2)}) collective-permute-start(bf16[128,128]{1,0:T(8,128)(2,1)S(1)} %get-tuple-element.78), channel_id=1, source_target_pairs={{0,12},{4,8},{8,4},{12,0},{16,28},{20,24},{24,20},{28,16},{1,13},{... | collective-permute-start | bytes 98312 | tf_op jit(solution)/shard_map/ppermute | solution.py:162
  43.7 7.7 %collective-permute-start.18 = (bf16[128,128]{1,0:T(8,128)(2,1)S(1)}, bf16[128,128]{1,0:T(8,128)(2,1)S(1)}, u32[]{:S(2)}, u32[]{:S(2)}) collective-permute-start(bf16[128,128]{1,0:T(8,128)(2,1)S(1)} %get-tuple-element.79), channel_id=1, source_target_pairs={{0,16},{4,20},{8,24},{12,28},{16,0},{20,4},{24,8},{28,12},{1,17},{... | collective-permute-start | bytes 98312 | tf_op jit(solution)/shard_map/ppermute | solution.py:162
  43.7 7.7 %collective-permute-start.19 = (bf16[128,128]{1,0:T(8,128)(2,1)S(1)}, bf16[128,128]{1,0:T(8,128)(2,1)S(1)}, u32[]{:S(2)}, u32[]{:S(2)}) collective-permute-start(bf16[128,128]{1,0:T(8,128)(2,1)S(1)} %get-tuple-element.80), channel_id=1, source_target_pairs={{0,20},{4,16},{8,28},{12,24},{16,4},{20,0},{24,12},{28,8},{1,21},{... | collective-permute-start | bytes 98312 | tf_op jit(solution)/shard_map/ppermute | solution.py:162
  46.6 5.7 %collective-permute-start.20 = (bf16[128,128]{1,0:T(8,128)(2,1)S(1)}, bf16[128,128]{1,0:T(8,128)(2,1)S(1)}, u32[]{:S(2)}, u32[]{:S(2)}) collective-permute-start(bf16[128,128]{1,0:T(8,128)(2,1)S(1)} %get-tuple-element.81), channel_id=1, source_target_pairs={{0,24},{4,28},{8,16},{12,20},{16,8},{20,12},{24,0},{28,4},{1,25},{... | collective-permute-start | bytes 98312 | tf_op jit(solution)/shard_map/ppermute | solution.py:162
  48.2 6.6 %collective-permute-start.21 = (bf16[128,128]{1,0:T(8,128)(2,1)S(1)}, bf16[128,128]{1,0:T(8,128)(2,1)S(1)}, u32[]{:S(2)}, u32[]{:S(2)}) collective-permute-start(bf16[128,128]{1,0:T(8,128)(2,1)S(1)} %get-tuple-element.82), channel_id=1, source_target_pairs={{0,28},{4,24},{8,20},{12,16},{16,12},{20,8},{24,4},{28,0},{1,29},{... | collective-permute-start | bytes 98312 | tf_op jit(solution)/shard_map/ppermute | solution.py:162
  63.5 6.5 %collective-permute-start.23 = (bf16[128,128]{1,0:T(8,128)(2,1)S(1)}, bf16[128,128]{1,0:T(8,128)(2,1)S(1)}, u32[]{:S(2)}, u32[]{:S(2)}) collective-permute-start(bf16[128,128]{1,0:T(8,128)(2,1)S(1)} %get-tuple-element.85), channel_id=1, source_target_pairs={{0,4},{4,0},{8,12},{12,8},{16,20},{20,16},{24,28},{28,24},{1,5},{5... | collective-permute-start | bytes 98312 | tf_op jit(solution)/shard_map/ppermute | solution.py:162
  64.1 9.0 %collective-permute-start.24 = (bf16[128,128]{1,0:T(8,128)(2,1)S(1)}, bf16[128,128]{1,0:T(8,128)(2,1)S(1)}, u32[]{:S(2)}, u32[]{:S(2)}) collective-permute-start(bf16[128,128]{1,0:T(8,128)(2,1)S(1)} %get-tuple-element.86), channel_id=1, source_target_pairs={{0,8},{4,12},{8,0},{12,4},{16,24},{20,28},{24,16},{28,20},{1,9},{5... | collective-permute-start | bytes 98312 | tf_op jit(solution)/shard_map/ppermute | solution.py:162
  64.1 11.2 %collective-permute-start.25 = (bf16[128,128]{1,0:T(8,128)(2,1)S(1)}, bf16[128,128]{1,0:T(8,128)(2,1)S(1)}, u32[]{:S(2)}, u32[]{:S(2)}) collective-permute-start(bf16[128,128]{1,0:T(8,128)(2,1)S(1)} %get-tuple-element.87), channel_id=1, source_target_pairs={{0,12},{4,8},{8,4},{12,0},{16,28},{20,24},{24,20},{28,16},{1,13},{... | collective-permute-start | bytes 98312 | tf_op jit(solution)/shard_map/ppermute | solution.py:162
  67.0 8.3 %collective-permute-start.26 = (bf16[128,128]{1,0:T(8,128)(2,1)S(1)}, bf16[128,128]{1,0:T(8,128)(2,1)S(1)}, u32[]{:S(2)}, u32[]{:S(2)}) collective-permute-start(bf16[128,128]{1,0:T(8,128)(2,1)S(1)} %get-tuple-element.88), channel_id=1, source_target_pairs={{0,16},{4,20},{8,24},{12,28},{16,0},{20,4},{24,8},{28,12},{1,17},{... | collective-permute-start | bytes 98312 | tf_op jit(solution)/shard_map/ppermute | solution.py:162
  67.8 7.6 %collective-permute-start.27 = (bf16[128,128]{1,0:T(8,128)(2,1)S(1)}, bf16[128,128]{1,0:T(8,128)(2,1)S(1)}, u32[]{:S(2)}, u32[]{:S(2)}) collective-permute-start(bf16[128,128]{1,0:T(8,128)(2,1)S(1)} %get-tuple-element.89), channel_id=1, source_target_pairs={{0,20},{4,16},{8,28},{12,24},{16,4},{20,0},{24,12},{28,8},{1,21},{... | collective-permute-start | bytes 98312 | tf_op jit(solution)/shard_map/ppermute | solution.py:162
  69.9 5.8 %collective-permute-start.28 = (bf16[128,128]{1,0:T(8,128)(2,1)S(1)}, bf16[128,128]{1,0:T(8,128)(2,1)S(1)}, u32[]{:S(2)}, u32[]{:S(2)}) collective-permute-start(bf16[128,128]{1,0:T(8,128)(2,1)S(1)} %get-tuple-element.90), channel_id=1, source_target_pairs={{0,24},{4,28},{8,16},{12,20},{16,8},{20,12},{24,0},{28,4},{1,25},{... | collective-permute-start | bytes 98312 | tf_op jit(solution)/shard_map/ppermute | solution.py:162
  73.1 6.6 %collective-permute-start.29 = (bf16[128,128]{1,0:T(8,128)(2,1)S(1)}, bf16[128,128]{1,0:T(8,128)(2,1)S(1)}, u32[]{:S(2)}, u32[]{:S(2)}) collective-permute-start(bf16[128,128]{1,0:T(8,128)(2,1)S(1)} %get-tuple-element.91), channel_id=1, source_target_pairs={{0,28},{4,24},{8,20},{12,16},{16,12},{20,8},{24,4},{28,0},{1,29},{... | collective-permute-start | bytes 98312 | tf_op jit(solution)/shard_map/ppermute | solution.py:162
  (12 other events, 128.1 us)

commit v4 on v0

v4 whole, which is shorter than its diff:
```python
import functools

import jax
import jax.numpy as jnp
from jax import lax
from jax.experimental import pallas as pl
from jax.experimental.pallas import tpu as pltpu
from jax.sharding import PartitionSpec as P

slot_group = 8
field = 10
field_mask = (1 << field) - 1
pairs = ((0, 1), (0, 2), (0, 3), (1, 2), (1, 3), (2, 3))
params = pltpu.CompilerParams(vmem_limit_bytes=24 * 1024 * 1024)
vmem = pl.BlockSpec(memory_space=pltpu.VMEM)
smem = pl.BlockSpec(memory_space=pltpu.SMEM)


def sibling_values(value, layers):
    cols = lax.axis_size("pcol")
    depth = lax.axis_size("zgrid")
    found = []
    for k in range(cols):
        if k == 0 and layers == 0:
            found.append(value)
            continue
        moves = []
        for c in range(cols):
            for z in range(depth):
                target = ((c - k) % cols) * depth + (z - layers) % depth
                moves.append((c * depth + z, target))
        found.append(lax.ppermute(value, ("pcol", "zgrid"), moves))
    return found


def from_other_core(value):
    return lax.ppermute(value, "zgrid", [(0, 1), (1, 0)])


def plan_kernel(row_count, cols, sources, targets, counts, plan):
    me = lax.axis_index("pcol")
    spare = row_count << field
    for level in range(3):
        first_list = pairs.index((level, level + 1))
        lists = 3 - level

        def one_slot(slot, found):
            target = targets[level, 0, slot]
            higher = [(target >= (level + j) * row_count).astype(jnp.int32) for j in range(1, lists)]
            step = sum(higher) if higher else jnp.int32(0)
            row = target - (level + step) * row_count
            column = sources[level, 0, slot] - me
            column = jnp.where(column < 0, column + cols, column)
            place = found[lists - 1]
            for j in range(lists - 1):
                place = jnp.where(step == j, found[j], place)
            plan[first_list + step, place] = (slot << (2 * field)) + (row << field) + column
            return tuple(found[j] + (step == j).astype(jnp.int32) for j in range(lists))

        found = lax.fori_loop(0, counts[level], one_slot, (jnp.int32(0),) * lists)
        for j in range(lists):
            plan[len(pairs), first_list + j] = found[j]
            for extra in range(slot_group):
                plan[first_list + j, found[j] + extra] = spare


def make_plan(row_count, cols, sources, targets, counts):
    width = -(-(sources.shape[-1] + slot_group) // 128) * 128
    return pl.pallas_call(
        functools.partial(plan_kernel, row_count, cols),
        out_shape=jax.ShapeDtypeStruct((8, width), jnp.int32),
        in_specs=[smem, smem, smem],
        out_specs=smem,
        compiler_params=params,
    )(sources, targets, counts)


def lanes_below(shape, count):
    return lax.broadcasted_iota(jnp.int32, shape, len(shape) - 1) < count


def turned(value):
    return pltpu.roll(value, value.shape[-1] // 2, value.ndim - 1)


def packed(value):
    half = value.shape[0] // 2
    low = lanes_below((half, value.shape[1]), value.shape[1] // 2)
    return jnp.where(low, value[:half], turned(value[half:]))


def unpacked(value):
    return jnp.concatenate([value, turned(value)], axis=0)


def half_first(value, half_index):
    return jnp.where(half_index == 0, value, turned(value))


def update_kernel(config, *refs):
    lists, layer_count, groups_of_solutions, cols, row_count, halved, form, carries, sends = config
    refs = list(refs)
    plans = [refs.pop(0) for _ in range(layer_count)]
    blocks = [refs.pop(0) for _ in range(layer_count)]
    solutions = [[refs.pop(0) for _ in range(cols)] for _ in range(groups_of_solutions)]
    total_in = refs.pop(0) if carries else None
    out, wide, total = refs
    width = blocks[0].shape[2]
    sides = out.shape[-1]
    chunks = wide.shape[2] // sides
    half_index = lax.axis_index("zgrid")
    low = lanes_below((width, sides), sides // 2)

    for j in range(groups_of_solutions):
        parts = [ref[...].astype(jnp.float32) for ref in solutions[j]]
        if not halved:
            for k in range(cols):
                wide[j, :, k * sides : (k + 1) * sides] = solutions[j][k][...]
            continue
        if form == "whole":
            parts = [half_first(part, half_index) for part in parts]
        else:
            parts = [unpacked(part) for part in parts]
        parts.append(parts[0])
        for k in range(chunks):
            both = jnp.where(low, parts[2 * k], turned(parts[2 * k + 1]))
            wide[j, :, k * sides : (k + 1) * sides] = both.astype(jnp.bfloat16)

    if carries:
        total[:row_count] = total_in[...]
    else:
        total[...] = jnp.zeros_like(total)

    for pair, layer, j in lists:
        plan = plans[layer]
        level = pairs[pair][0]

        def one_group(g, unused):
            entries = [plan[pair, g * slot_group + s] for s in range(slot_group)]
            pieces = [
                blocks[layer][level, lax.shift_right_logical(e, 2 * field)] for e in entries
            ]
            product = jnp.dot(
                jnp.concatenate(pieces, axis=0), wide[j], preferred_element_type=jnp.float32
            )
            for s in range(slot_group):
                place = lax.shift_right_logical(entries[s], field) & field_mask
                column = entries[s] & field_mask
                chunk = lax.shift_right_logical(column, 1) if halved else column
                rows = product[s * width : (s + 1) * width]
                part = rows[:, :sides]
                for k in range(1, chunks):
                    part = jnp.where(chunk == k, rows[:, k * sides : (k + 1) * sides], part)
                if halved:
                    part = jnp.where(low == ((column & 1) == 0), part, 0.0)
                total[place] += part
            return unused

        live = plan[len(pairs), pair]
        lax.fori_loop(0, (live + slot_group - 1) // slot_group, one_group, 0)

    if not sends:
        out[...] = total[:row_count]
    elif not halved:
        out[...] = total[:row_count].astype(jnp.bfloat16)
    else:
        for row in range(row_count):
            value = total[row]
            out[row] = packed(value + turned(value)).astype(jnp.bfloat16)


def update(lists, layers, solution_groups, form, total_in, row_count, halved, sends):
    cols = len(solution_groups[0])
    width = layers[0][1].shape[2]
    sides = solution_groups[0][0].shape[-1]
    solutions = [part for group in solution_groups for part in group]
    operands = [a[0] for a in layers] + [a[1] for a in layers] + solutions
    specs = [smem] * len(layers) + [vmem] * (len(layers) + len(solutions))
    if total_in is not None:
        operands.append(total_in)
        specs.append(vmem)
    if sends:
        rows = width // 2 if halved else width
        out_shape = jax.ShapeDtypeStruct((row_count, rows, sides), jnp.bfloat16)
    else:
        out_shape = jax.ShapeDtypeStruct((row_count, width, sides), jnp.float32)
    chunks = (cols + 1) // 2 if halved else cols
    config = (
        lists, len(layers), len(solution_groups), cols, row_count, halved, form,
        total_in is not None, sends,
    )
    return pl.pallas_call(
        functools.partial(update_kernel, config),
        out_shape=out_shape,
        in_specs=specs,
        out_specs=vmem,
        scratch_shapes=[
            pltpu.VMEM((len(solution_groups), width, chunks * sides), jnp.bfloat16),
            pltpu.VMEM((row_count + 1, width, sides), jnp.float32),
        ],
        compiler_params=params,
    )(*operands)


def half_solve_kernel(level, received, given, inverse, *refs):
    earlier, out = refs if len(refs) == 2 else (None, refs[0])
    half_index = lax.axis_index("zgrid")
    incoming = received[0].astype(jnp.float32)
    for row in range(1, received.shape[0]):
        incoming = incoming + received[row].astype(jnp.float32)
    right = half_first(given[level].astype(jnp.float32), half_index)
    residual = (right - unpacked(incoming)).astype(jnp.bfloat16)
    solved = packed(jnp.dot(inverse[level], residual, preferred_element_type=jnp.float32))
    if earlier is None:
        out[...] = solved.astype(jnp.bfloat16)
    else:
        out[0] = earlier[...]
        out[1] = solved.astype(jnp.bfloat16)


def half_solve(level, received, given, inverse, earlier):
    shape = received.shape[1:]
    operands = [received, given, inverse] + ([] if earlier is None else [earlier])
    return pl.pallas_call(
        functools.partial(half_solve_kernel, level),
        out_shape=jax.ShapeDtypeStruct(shape if earlier is None else (2,) + shape, jnp.bfloat16),
        in_specs=[vmem] * len(operands),
        out_specs=vmem,
        compiler_params=params,
    )(*operands)


def join_kernel(own, other, out):
    half_index = lax.axis_index("zgrid")
    for level in range(2):
        mine = own[level].astype(jnp.float32)
        theirs = other[level].astype(jnp.float32)
        first = unpacked(jnp.where(half_index == 0, mine, theirs))
        second = unpacked(jnp.where(half_index == 0, theirs, mine))
        low = lanes_below(first.shape, first.shape[-1] // 2)
        out[0, 0, level] = jnp.where(low, first, turned(second)).astype(jnp.bfloat16)


def join_halves(own, other):
    levels, half, sides = own.shape
    return pl.pallas_call(
        join_kernel,
        out_shape=jax.ShapeDtypeStruct((1, 1, levels, 2 * half, sides), jnp.bfloat16),
        in_specs=[vmem, vmem],
        out_specs=vmem,
        compiler_params=params,
    )(own, other)


def solve_block(inverse, residual):
    return jnp.dot(inverse, residual, preferred_element_type=jnp.float32).astype(jnp.bfloat16)


def exchange(send):
    return lax.all_to_all(send, "prow", 0, 0, tiled=True)


def local(blocks, sources, targets, counts, given_sub, given_top, inverse_sub, inverse_top):
    row_count = lax.axis_size("prow")
    cols = lax.axis_size("pcol")
    levels, capacity = sources.shape[3:]
    block_set = blocks[0, 0, 0]
    right_sub = given_sub[0, 0, 0]
    factor_sub = inverse_sub[0, 0, 0]
    right_top = given_top[0, 0]
    factor_top = inverse_top[0, 0]

    level_zero = solve_block(factor_sub[0], right_sub[0])
    zero_own = sibling_values(level_zero, 0)
    zero_other = sibling_values(level_zero, 1)
    plan = make_plan(
        row_count, cols,
        sources.reshape(levels, 1, capacity), targets.reshape(levels, 1, capacity),
        counts.reshape(levels),
    )
    block_other = from_other_core(block_set)
    plan_other = from_other_core(plan)
    own = (plan, block_set)
    other = (plan_other, block_other)

    send = update([(0, 0, 0)], [own], [zero_own], "whole", None, row_count, False, True)
    send, zero_other, plan_other = lax.optimization_barrier((send, zero_other, plan_other))
    other = (plan_other, block_other)
    received = exchange(send)
    second = update(
        [(1, 0, 0), (1, 1, 1)], [own, other], [zero_own, zero_other], "whole", None,
        row_count, True, False,
    )
    received, second = lax.optimization_barrier((received, second))
    incoming = jnp.sum(received.astype(jnp.float32), axis=0)
    level_one = solve_block(
        factor_sub[1], (right_sub[1].astype(jnp.float32) - incoming).astype(jnp.bfloat16)
    )
    one_own = sibling_values(level_one, 0)
    one_other = sibling_values(level_one, 1)

    send = update(
        [(3, 0, 0), (3, 1, 1)], [own, other], [one_own, one_other], "whole", second,
        row_count, True, True,
    )
    received = exchange(send)
    third = update(
        [(2, 0, 0), (2, 1, 1), (4, 0, 2), (4, 1, 3)], [own, other],
        [zero_own, zero_other, one_own, one_other], "whole", None, row_count, True, False,
    )
    received, third = lax.optimization_barrier((received, third))
    level_two = half_solve(0, received, right_top, factor_top, None)
    two_own = sibling_values(level_two, 0)

    send = update(
        [(5, 0, 0), (5, 1, 0)], [own, other], [two_own], "packed", third, row_count, True, True
    )
    solved_halves = half_solve(1, exchange(send), right_top, factor_top, level_two)
    solved_top = join_halves(solved_halves, from_other_core(solved_halves))
    solved_sub = jnp.stack([level_zero, level_one])[None, None, None]
    return (solved_sub, solved_top)


def solution(mesh):
    in_specs = (
        P("prow", "pcol", "zgrid", None, None, None, None),
        P("prow", "pcol", "zgrid", None, None),
        P("prow", "pcol", "zgrid", None, None),
        P("prow", "pcol", "zgrid", None),
        P("prow", "pcol", "zgrid", None, None, None),
        P("prow", "pcol", None, None, None),
        P("prow", "pcol", "zgrid", None, None, None),
        P("prow", "pcol", None, None, None),
    )
    out_specs = (P("prow", "pcol", "zgrid", None, None, None), P("prow", "pcol", None, None, None))
    return jax.shard_map(local, mesh=mesh, in_specs=in_specs, out_specs=out_specs, check_vma=False)
```

time: 283 us -> 77.4 us (0.27)
  waiting for transfers between devices: 201 us -> 11.3 us
  Pallas kernels: 0 us -> 19.6 us
  starting transfers between devices: 0.12 us -> 17.9 us
  between operations: 15.8 us -> 0.75 us
  other arithmetic: 15.3 us -> 0.68 us
  matrix products: 11.4 us -> 1.03 us
  blocking collectives: 22.8 us -> 12.8 us
    reduce_scatter x3 -> x0, waiting for transfers between devices: 201 us -> none  [reduce_rows(): lax.psum_scatter(section.astype(jnp.bfloat16), 'prow', scatter_dimension=...]
    pallas_call x0 -> x9, Pallas kernels: none -> 19.6 us  [the longest x5 16.2 us: update(): pl.pallas_call(functools.partial(update_kernel, config), out_shape=out_sh...]
    all_gather x3 -> x0, blocking collectives: 14.7 us -> none  [spread_updates(): gathered = lax.all_gather(solved[None], 'pcol', axis=0, tiled=True)]
    all_to_all x0 -> x1, blocking collectives: none -> 12.8 us  [exchange(): return lax.all_to_all(send, 'prow', 0, 0, tiled=True)]
    unnamed x13 -> x24, local copies, waits for them, and re-layouts: 0.78 us -> 12.6 us
    all_to_all x0 -> x2, starting transfers between devices: none -> 10.5 us  [exchange(): return lax.all_to_all(send, 'prow', 0, 0, tiled=True)]
    dot_general x8 -> x0, matrix products: 10 us -> none  [add_group(): jnp.einsum('swk,skr->swr', block_piece, chosen, preferred_element_type=jn...]
    scatter-add x8 -> x0, other arithmetic: 8.25 us -> none  [add_group(): return running.at[target_part].add(product)]
  transfers between devices with their start and end apart: 3 -> 12, of which waited for: 3 -> 6; matrix products, arithmetic and copies ran while one was open for 0% -> 2% of each run, Pallas kernels for 0% -> 13%
where the time goes in v4:
time: 77.4 us; the launch traced here: 76.6 us
  Pallas kernels  19.6 us (25%)
  starting transfers between devices  17.9 us (23%)
  blocking collectives  12.8 us (17%)
  local copies, waits for them, and re-layouts  12.6 us (16%)
  waiting for transfers between devices  11.3 us (15%)
  matrix products  1.03 us (1%)
    pallas_call x5, Pallas kernels, update(): pl.pallas_call(functools.partial(update_kernel, config), out_shape=out_sh...  16.2 us
    all_to_all x1, blocking collectives, exchange(): return lax.all_to_all(send, 'prow', 0, 0, tiled=True)  12.8 us
    unnamed x24, local copies, waits for them, and re-layouts  12.6 us
    all_to_all x2, starting transfers between devices, exchange(): return lax.all_to_all(send, 'prow', 0, 0, tiled=True)  10.5 us
    ppermute x7, starting transfers between devices, sibling_values(): found.append(lax.ppermute(value, ('pcol', 'zgrid'), moves))  6.27 us
    all_to_all x2, waiting for transfers between devices, exchange(): return lax.all_to_all(send, 'prow', 0, 0, tiled=True)  5.93 us
    ppermute x7, waiting for transfers between devices, sibling_values(): found.append(lax.ppermute(value, ('pcol', 'zgrid'), moves))  4.79 us
    pallas_call x1, Pallas kernels, make_plan(): pl.pallas_call(functools.partial(plan_kernel, row_count, cols), out_shape...  1.99 us
  transfers between devices with their start and end apart: 12, of which 6 were waited for; matrix products, arithmetic and copies ran while one was open for 2% of the time, Pallas kernels for 13%

profile of v4, /device:TPU:0, one launch (start us, length us, event | category | flops | bytes accessed | tf_op | source)
XLA Modules:
  0.0 76.6 jit_solution(13048060603686855309)
XLA Ops:
  1.1 0.9 %convolution_convert_fusion.1.refs_2_.refs_4_ = bf16[128,128]{1,0:T(8,128)(2,1)S(1)} fusion(bf16[1,1,1,2,128,128]{5,4,3,2,1,0:T(8,128)(2,1)} %param.12, bf16[1,1,1,2,128,128]{5,4,3,2,1,0:T(8,128)(2,1)} %param.14), kind=kOutput, calls=%fused_computation.1 | convolution fusion | flops 4210688 | bytes 98304 | tf_op jit(solution)/shard_map/dot_general | solution.py:256
  2.0 2.6 %collective-permute-start = (bf16[128,128]{1,0:T(8,128)(2,1)S(1)}, bf16[128,128]{1,0:T(8,128)(2,1)S(1)}, u32[]{:S(2)}, u32[]{:S(2)}) collective-permute-start(bf16[128,128]{1,0:T(8,128)(2,1)S(1)} %convolution_convert_fusion.1.refs_2_.refs_4_), channel_id=1, source_target_pairs={{0,2},{1,3},{2,0},{3,1},{4,6},{5,7},{6,4},{7,5},{8,10},{9,11},{10,... | collective-permute-start | bytes 98312 | tf_op jit(solution)/shard_map/ppermute | solution.py:32
  6.8 2.0 %shard_map.95.refs_0_ = s32[8,128]{1,0:T(8,128)S(1)} custom-call(s32[3,1,40]{2,1,0:T(1,128)S(1)} %bitcast.48, s32[3,1,40]{2,1,0:T(1,128)S(1)} %bitcast.49, s32[3]{0:T(128)S(1)} %bitcast.50), custom_call_target="tpu_custom_call" | custom-call | tf_op jit(solution)/shard_map/pallas_call | solution.py:69
  9.4 2.1 %copy-done = bf16[1,1,1,3,40,128,128]{6,5,4,3,2,1,0:T(8,128)(2,1)S(1)} copy-done((bf16[1,1,1,3,40,128,128]{6,5,4,3,2,1,0:T(8,128)(2,1)S(1)}, bf16[1,1,1,3,40,128,128]{6,5,4,3,2,1,0:T(8,128)(2,1)}, u32[]{:S(2)}) %copy-start) | copy-done | bytes 3932184
  11.5 1.4 %shard_map.96 = bf16[8,128,128]{2,1,0:T(8,128)(2,1)} custom-call(s32[8,128]{1,0:T(8,128)S(1)} %shard_map.95.refs_0_, bf16[3,40,128,128]{3,2,1,0:T(8,128)(2,1)S(1)} %bitcast.32, bf16[128,128]{1,0:T(8,128)(2,1)S(1)} %convolution_convert_fusion.1.refs_2_.refs_4_, bf16[128,128]{1,0:T(8,128)(2,1)S(1)} %collective-permute-done.refs_3_.refs_5_), custom_call_target="tpu_custom_call" | custom-call | tf_op jit(solution)/shard_map/pallas_call | solution.py:192
  12.9 7.1 %all-to-all-start = ((bf16[8,128,128]{2,1,0:T(8,128)(2,1)}), bf16[8,128,128]{2,1,0:T(8,128)(2,1)S(1)}, u32[]{:S(2)}, u32[]{:S(2)}) async-start(bf16[8,128,128]{2,1,0:T(8,128)(2,1)} %shard_map.96), calls=%async_computation | async-start | bytes 524288 | tf_op jit(solution)/shard_map/all_to_all | solution.py:260
  20.0 2.1 %copy-done.1 = bf16[1,1,1,3,40,128,128]{6,5,4,3,2,1,0:T(8,128)(2,1)S(1)} copy-done((bf16[1,1,1,3,40,128,128]{6,5,4,3,2,1,0:T(8,128)(2,1)S(1)}, bf16[1,1,1,3,40,128,128]{6,5,4,3,2,1,0:T(8,128)(2,1)}, u32[]{:S(2)}) %copy-start.1) | copy-done | bytes 3932184
  22.1 2.9 %shard_map.97.refs_8_ = f32[8,128,128]{2,1,0:T(8,128)S(1)} custom-call(s32[8,128]{1,0:T(8,128)S(1)} %shard_map.95.refs_0_, s32[8,128]{1,0:T(8,128)S(1)} %collective-permute-done.3.refs_1_, bf16[3,40,128,128]{3,2,1,0:T(8,128)(2,1)S(1)} %bitcast.33, bf16[3,40,128,128]{3,2,1,0:T(8,128)(2,1)} %collective-permute-done.4.refs_3_, ...), custom_call_target="tpu_custom_call" | custom-call | tf_op jit(solution)/shard_map/pallas_call | solution.py:192
  25.0 4.4 %all-to-all-done = bf16[8,128,128]{2,1,0:T(8,128)(2,1)S(1)} async-done(((bf16[8,128,128]{2,1,0:T(8,128)(2,1)}), bf16[8,128,128]{2,1,0:T(8,128)(2,1)S(1)}, u32[]{:S(2)}, u32[]{:S(2)}) %all-to-all-start) | async-done | bytes 262176 | tf_op jit(solution)/shard_map/all_to_all | solution.py:260
  30.2 1.6 %collective-permute-start.5 = (bf16[128,128]{1,0:T(8,128)(2,1)S(1)}, bf16[128,128]{1,0:T(8,128)(2,1)S(1)}, u32[]{:S(2)}, u32[]{:S(2)}) collective-permute-start(bf16[128,128]{1,0:T(8,128)(2,1)S(1)} %bitcast.40), channel_id=1, source_target_pairs={{0,2},{1,3},{2,0},{3,1},{4,6},{5,7},{6,4},{7,5},{8,10},{9,11},{10,... | collective-permute-start | bytes 98312 | tf_op jit(solution)/shard_map/ppermute | solution.py:32
  31.8 1.2 %collective-permute-done.7.refs_7_.refs_11_ = bf16[128,128]{1,0:T(8,128)(2,1)S(1)} collective-permute-done((bf16[128,128]{1,0:T(8,128)(2,1)S(1)}, bf16[128,128]{1,0:T(8,128)(2,1)S(1)}, u32[]{:S(2)}, u32[]{:S(2)}) %collective-permute-start.7) | collective-permute-done | bytes 32800 | tf_op jit(solution)/shard_map/ppermute | solution.py:32
  33.0 1.1 %collective-permute-done.5.refs_5_.refs_9_ = bf16[128,128]{1,0:T(8,128)(2,1)S(1)} collective-permute-done((bf16[128,128]{1,0:T(8,128)(2,1)S(1)}, bf16[128,128]{1,0:T(8,128)(2,1)S(1)}, u32[]{:S(2)}, u32[]{:S(2)}) %collective-permute-start.5) | collective-permute-done | bytes 32800 | tf_op jit(solution)/shard_map/ppermute | solution.py:32
  34.1 2.1 %copy-done.2 = bf16[1,1,1,3,40,128,128]{6,5,4,3,2,1,0:T(8,128)(2,1)S(1)} copy-done((bf16[1,1,1,3,40,128,128]{6,5,4,3,2,1,0:T(8,128)(2,1)S(1)}, bf16[1,1,1,3,40,128,128]{6,5,4,3,2,1,0:T(8,128)(2,1)}, u32[]{:S(2)}) %copy-start.2) | copy-done | bytes 3932184
  36.2 4.4 %shard_map.98 = bf16[8,64,128]{2,1,0:T(8,128)(2,1)} custom-call(s32[8,128]{1,0:T(8,128)S(1)} %shard_map.95.refs_0_, s32[8,128]{1,0:T(8,128)S(1)} %collective-permute-done.3.refs_1_, bf16[3,40,128,128]{3,2,1,0:T(8,128)(2,1)S(1)} %bitcast.34, bf16[3,40,128,128]{3,2,1,0:T(8,128)(2,1)} %collective-permute-done.4.refs_3_, bf16[128,128]{1,0:T(8,128)(2,1)S(1)} %bitcast.41, ...), custom_call_target="tpu_custom_call" | custom-call | tf_op jit(solution)/shard_map/pallas_call | solution.py:192
  40.6 3.4 %all-to-all-start.1 = ((bf16[8,64,128]{2,1,0:T(8,128)(2,1)}), bf16[8,64,128]{2,1,0:T(8,128)(2,1)S(1)}, u32[]{:S(2)}, u32[]{:S(2)}) async-start(bf16[8,64,128]{2,1,0:T(8,128)(2,1)} %shard_map.98), calls=%async_computation.1 | async-start | bytes 262144 | tf_op jit(solution)/shard_map/all_to_all | solution.py:260
  44.0 2.1 %copy-done.3 = bf16[1,1,1,3,40,128,128]{6,5,4,3,2,1,0:T(8,128)(2,1)S(1)} copy-done((bf16[1,1,1,3,40,128,128]{6,5,4,3,2,1,0:T(8,128)(2,1)S(1)}, bf16[1,1,1,3,40,128,128]{6,5,4,3,2,1,0:T(8,128)(2,1)}, u32[]{:S(2)}) %copy-start.3) | copy-done | bytes 3932184
  46.1 3.7 %shard_map.99.refs_6_ = f32[8,128,128]{2,1,0:T(8,128)S(1)} custom-call(s32[8,128]{1,0:T(8,128)S(1)} %shard_map.95.refs_0_, s32[8,128]{1,0:T(8,128)S(1)} %collective-permute-done.3.refs_1_, bf16[3,40,128,128]{3,2,1,0:T(8,128)(2,1)S(1)} %bitcast.35, bf16[3,40,128,128]{3,2,1,0:T(8,128)(2,1)} %collective-permute-done.4.refs_3_, ...), custom_call_target="tpu_custom_call" | custom-call | tf_op jit(solution)/shard_map/pallas_call | solution.py:192
  49.8 1.5 %all-to-all-done.1.received = bf16[8,64,128]{2,1,0:T(8,128)(2,1)S(1)} async-done(((bf16[8,64,128]{2,1,0:T(8,128)(2,1)}), bf16[8,64,128]{2,1,0:T(8,128)(2,1)S(1)}, u32[]{:S(2)}, u32[]{:S(2)}) %all-to-all-start.1) | async-done | bytes 131104 | tf_op jit(solution)/shard_map/all_to_all | solution.py:260
  51.6 1.3 %collective-permute-start.8 = (bf16[64,128]{1,0:T(8,128)(2,1)S(1)}, bf16[64,128]{1,0:T(8,128)(2,1)S(1)}, u32[]{:S(2)}, u32[]{:S(2)}) collective-permute-start(bf16[64,128]{1,0:T(8,128)(2,1)S(1)} %shard_map.100.refs_4_.refs_0_), channel_id=1, source_target_pairs={{0,2},{1,3},{2,0},{3,1},{4,6},{5,7},{6,4},{7,5},{8,10},{9,11},{10,... | collective-permute-start | bytes 49160 | tf_op jit(solution)/shard_map/ppermute | solution.py:32
  52.9 2.4 %collective-permute-done.8.refs_5_ = bf16[64,128]{1,0:T(8,128)(2,1)S(1)} collective-permute-done((bf16[64,128]{1,0:T(8,128)(2,1)S(1)}, bf16[64,128]{1,0:T(8,128)(2,1)S(1)}, u32[]{:S(2)}, u32[]{:S(2)}) %collective-permute-start.8) | collective-permute-done | bytes 16416 | tf_op jit(solution)/shard_map/ppermute | solution.py:32
  55.4 2.1 %copy-done.4 = bf16[1,1,1,3,40,128,128]{6,5,4,3,2,1,0:T(8,128)(2,1)S(1)} copy-done((bf16[1,1,1,3,40,128,128]{6,5,4,3,2,1,0:T(8,128)(2,1)S(1)}, bf16[1,1,1,3,40,128,128]{6,5,4,3,2,1,0:T(8,128)(2,1)}, u32[]{:S(2)}) %copy-start.4) | copy-done | bytes 3932184
  57.5 3.9 %shard_map.101 = bf16[8,64,128]{2,1,0:T(8,128)(2,1)S(1)} custom-call(s32[8,128]{1,0:T(8,128)S(1)} %shard_map.95.refs_0_, s32[8,128]{1,0:T(8,128)S(1)} %collective-permute-done.3.refs_1_, bf16[3,40,128,128]{3,2,1,0:T(8,128)(2,1)S(1)} %bitcast.36, bf16[3,40,128,128]{3,2,1,0:T(8,128)(2,1)} %collective-permute-done.4.refs_3_, ...), custom_call_target="tpu_custom_call" | custom-call | tf_op jit(solution)/shard_map/pallas_call | solution.py:192
  61.4 12.8 %all_to_all.15.received = bf16[8,64,128]{2,1,0:T(8,128)(2,1)S(1)} all-to-all(bf16[8,64,128]{2,1,0:T(8,128)(2,1)S(1)} %shard_map.101), channel_id=1, replica_groups=mesh['prow'=8,'pcol'=2,'zgrid'=2] {'prow'}, dimensions={0} | all-to-all | bytes 262144 | tf_op jit(solution)/shard_map/all_to_all | solution.py:260
  75.8 0.8 %shard_map.103 = bf16[1,1,2,128,128]{4,3,2,1,0:T(8,128)(2,1)} custom-call(bf16[2,64,128]{2,1,0:T(8,128)(2,1)S(1)} %shard_map.102.own, bf16[2,64,128]{2,1,0:T(8,128)(2,1)S(1)} %collective-permute-done.9.other), custom_call_target="tpu_custom_call" | custom-call | tf_op jit(solution)/shard_map/pallas_call | solution.py:246
  (38 shorter events, 5.9 us)
Async XLA Ops:
  0.6 19.4 %collective-permute-start.4 = (bf16[3,40,128,128]{3,2,1,0:T(8,128)(2,1)}, bf16[3,40,128,128]{3,2,1,0:T(8,128)(2,1)}, u32[]{:S(2)}, u32[]{:S(2)}) collective-permute-start(bf16[3,40,128,128]{3,2,1,0:T(8,128)(2,1)} %bitcast.31), channel_id=1, source_target_pairs={{0,1},{1,0},{2,3},{3,2},{4,5},{5,4},{6,7},{7,6},{8,9},{9,8},{10,11... | collective-permute-start | bytes 11796488 | tf_op jit(solution)/shard_map/ppermute | solution.py:37
  2.0 7.3 %collective-permute-start = (bf16[128,128]{1,0:T(8,128)(2,1)S(1)}, bf16[128,128]{1,0:T(8,128)(2,1)S(1)}, u32[]{:S(2)}, u32[]{:S(2)}) collective-permute-start(bf16[128,128]{1,0:T(8,128)(2,1)S(1)} %convolution_convert_fusion.1.refs_2_.refs_4_), channel_id=1, source_target_pairs={{0,2},{1,3},{2,0},{3,1},{4,6},{5,7},{6,4},{7,5},{8,10},{9,11},{10,... | collective-permute-start | bytes 98312 | tf_op jit(solution)/shard_map/ppermute | solution.py:32
  4.6 8.3 %collective-permute-start.2 = (bf16[128,128]{1,0:T(8,128)(2,1)S(1)}, bf16[128,128]{1,0:T(8,128)(2,1)S(1)}, u32[]{:S(2)}, u32[]{:S(2)}) collective-permute-start(bf16[128,128]{1,0:T(8,128)(2,1)S(1)} %convolution_convert_fusion.1.refs_2_.refs_4_), channel_id=1, source_target_pairs={{0,3},{1,2},{2,1},{3,0},{4,7},{5,6},{6,5},{7,4},{8,11},{9,10},{10,... | collective-permute-start | bytes 98312 | tf_op jit(solution)/shard_map/ppermute | solution.py:32
  4.8 8.1 %collective-permute-start.1 = (bf16[128,128]{1,0:T(8,128)(2,1)S(1)}, bf16[128,128]{1,0:T(8,128)(2,1)S(1)}, u32[]{:S(2)}, u32[]{:S(2)}) collective-permute-start(bf16[128,128]{1,0:T(8,128)(2,1)S(1)} %convolution_convert_fusion.1.refs_2_.refs_4_), channel_id=1, source_target_pairs={{0,1},{1,0},{2,3},{3,2},{4,5},{5,4},{6,7},{7,6},{8,9},{9,8},{10,11... | collective-permute-start | bytes 98312 | tf_op jit(solution)/shard_map/ppermute | solution.py:32
  4.8 0.7 copy-start.7
  5.5 0.7 copy-start.8
  6.2 0.7 copy-start.9
  8.9 4.0 %collective-permute-start.3 = (s32[8,128]{1,0:T(8,128)S(1)}, s32[8,128]{1,0:T(8,128)S(1)}, u32[]{:S(2)}, u32[]{:S(2)}) collective-permute-start(s32[8,128]{1,0:T(8,128)S(1)} %shard_map.95.refs_0_), channel_id=1, source_target_pairs={{0,1},{1,0},{2,3},{3,2},{4,5},{5,4},{6,7},{7,6},{8,9},{9,8},{10,11... | collective-permute-start | bytes 12296 | tf_op jit(solution)/shard_map/ppermute | solution.py:37
  9.4 2.1 %copy-start = (bf16[1,1,1,3,40,128,128]{6,5,4,3,2,1,0:T(8,128)(2,1)S(1)}, bf16[1,1,1,3,40,128,128]{6,5,4,3,2,1,0:T(8,128)(2,1)}, u32[]{:S(2)}) copy-start(bf16[1,1,1,3,40,128,128]{6,5,4,3,2,1,0:T(8,128)(2,1)} %param.8) | copy-start | bytes 11796484
  12.9 16.5 %all-to-all-start = ((bf16[8,128,128]{2,1,0:T(8,128)(2,1)}), bf16[8,128,128]{2,1,0:T(8,128)(2,1)S(1)}, u32[]{:S(2)}, u32[]{:S(2)}) async-start(bf16[8,128,128]{2,1,0:T(8,128)(2,1)} %shard_map.96), calls=%async_computation | async-start | bytes 524288 | tf_op jit(solution)/shard_map/all_to_all | solution.py:260
  20.0 2.1 %copy-start.1 = (bf16[1,1,1,3,40,128,128]{6,5,4,3,2,1,0:T(8,128)(2,1)S(1)}, bf16[1,1,1,3,40,128,128]{6,5,4,3,2,1,0:T(8,128)(2,1)}, u32[]{:S(2)}) copy-start(bf16[1,1,1,3,40,128,128]{6,5,4,3,2,1,0:T(8,128)(2,1)} %param.8) | copy-start | bytes 11796484
  22.1 7.3 %copy-start.10 = (bf16[1,1,1,2,128,128]{5,4,3,2,1,0:T(8,128)(2,1)S(1)}, bf16[1,1,1,2,128,128]{5,4,3,2,1,0:T(8,128)(2,1)}, u32[]{:S(2)}) copy-start(bf16[1,1,1,2,128,128]{5,4,3,2,1,0:T(8,128)(2,1)} %param.12) | copy-start | bytes 196612
  22.1 7.3 %copy-start.11 = (bf16[1,1,1,2,128,128]{5,4,3,2,1,0:T(8,128)(2,1)S(1)}, bf16[1,1,1,2,128,128]{5,4,3,2,1,0:T(8,128)(2,1)}, u32[]{:S(2)}) copy-start(bf16[1,1,1,2,128,128]{5,4,3,2,1,0:T(8,128)(2,1)} %param.14) | copy-start | bytes 196612
  29.6 3.4 %collective-permute-start.7 = (bf16[128,128]{1,0:T(8,128)(2,1)S(1)}, bf16[128,128]{1,0:T(8,128)(2,1)S(1)}, u32[]{:S(2)}, u32[]{:S(2)}) collective-permute-start(bf16[128,128]{1,0:T(8,128)(2,1)S(1)} %bitcast.38), channel_id=1, source_target_pairs={{0,3},{1,2},{2,1},{3,0},{4,7},{5,6},{6,5},{7,4},{8,11},{9,10},{10,... | collective-permute-start | bytes 98312 | tf_op jit(solution)/shard_map/ppermute | solution.py:32
  29.6 3.3 %collective-permute-start.6 = (bf16[128,128]{1,0:T(8,128)(2,1)S(1)}, bf16[128,128]{1,0:T(8,128)(2,1)S(1)}, u32[]{:S(2)}, u32[]{:S(2)}) collective-permute-start(bf16[128,128]{1,0:T(8,128)(2,1)S(1)} %bitcast.39), channel_id=1, source_target_pairs={{0,1},{1,0},{2,3},{3,2},{4,5},{5,4},{6,7},{7,6},{8,9},{9,8},{10,11... | collective-permute-start | bytes 98312 | tf_op jit(solution)/shard_map/ppermute | solution.py:32
  30.2 3.9 %collective-permute-start.5 = (bf16[128,128]{1,0:T(8,128)(2,1)S(1)}, bf16[128,128]{1,0:T(8,128)(2,1)S(1)}, u32[]{:S(2)}, u32[]{:S(2)}) collective-permute-start(bf16[128,128]{1,0:T(8,128)(2,1)S(1)} %bitcast.40), channel_id=1, source_target_pairs={{0,2},{1,3},{2,0},{3,1},{4,6},{5,7},{6,4},{7,5},{8,10},{9,11},{10,... | collective-permute-start | bytes 98312 | tf_op jit(solution)/shard_map/ppermute | solution.py:32
  34.1 2.1 %copy-start.2 = (bf16[1,1,1,3,40,128,128]{6,5,4,3,2,1,0:T(8,128)(2,1)S(1)}, bf16[1,1,1,3,40,128,128]{6,5,4,3,2,1,0:T(8,128)(2,1)}, u32[]{:S(2)}) copy-start(bf16[1,1,1,3,40,128,128]{6,5,4,3,2,1,0:T(8,128)(2,1)} %param.8) | copy-start | bytes 11796484
  40.6 10.7 %all-to-all-start.1 = ((bf16[8,64,128]{2,1,0:T(8,128)(2,1)}), bf16[8,64,128]{2,1,0:T(8,128)(2,1)S(1)}, u32[]{:S(2)}, u32[]{:S(2)}) async-start(bf16[8,64,128]{2,1,0:T(8,128)(2,1)} %shard_map.98), calls=%async_computation.1 | async-start | bytes 262144 | tf_op jit(solution)/shard_map/all_to_all | solution.py:260
  44.0 2.1 %copy-start.3 = (bf16[1,1,1,3,40,128,128]{6,5,4,3,2,1,0:T(8,128)(2,1)S(1)}, bf16[1,1,1,3,40,128,128]{6,5,4,3,2,1,0:T(8,128)(2,1)}, u32[]{:S(2)}) copy-start(bf16[1,1,1,3,40,128,128]{6,5,4,3,2,1,0:T(8,128)(2,1)} %param.8) | copy-start | bytes 11796484
  46.1 5.2 %copy-start.5 = (bf16[1,1,2,128,128]{4,3,2,1,0:T(8,128)(2,1)S(1)}, bf16[1,1,2,128,128]{4,3,2,1,0:T(8,128)(2,1)}, u32[]{:S(2)}) copy-start(bf16[1,1,2,128,128]{4,3,2,1,0:T(8,128)(2,1)} %param.13) | copy-start | bytes 196612
  46.1 5.2 %copy-start.6 = (bf16[1,1,2,128,128]{4,3,2,1,0:T(8,128)(2,1)S(1)}, bf16[1,1,2,128,128]{4,3,2,1,0:T(8,128)(2,1)}, u32[]{:S(2)}) copy-start(bf16[1,1,2,128,128]{4,3,2,1,0:T(8,128)(2,1)} %param.15) | copy-start | bytes 196612
  51.6 3.8 %collective-permute-start.8 = (bf16[64,128]{1,0:T(8,128)(2,1)S(1)}, bf16[64,128]{1,0:T(8,128)(2,1)S(1)}, u32[]{:S(2)}, u32[]{:S(2)}) collective-permute-start(bf16[64,128]{1,0:T(8,128)(2,1)S(1)} %shard_map.100.refs_4_.refs_0_), channel_id=1, source_target_pairs={{0,2},{1,3},{2,0},{3,1},{4,6},{5,7},{6,4},{7,5},{8,10},{9,11},{10,... | collective-permute-start | bytes 49160 | tf_op jit(solution)/shard_map/ppermute | solution.py:32
  55.4 2.1 %copy-start.4 = (bf16[1,1,1,3,40,128,128]{6,5,4,3,2,1,0:T(8,128)(2,1)S(1)}, bf16[1,1,1,3,40,128,128]{6,5,4,3,2,1,0:T(8,128)(2,1)}, u32[]{:S(2)}) copy-start(bf16[1,1,1,3,40,128,128]{6,5,4,3,2,1,0:T(8,128)(2,1)} %param.8) | copy-start | bytes 11796484
  74.5 1.2 %collective-permute-start.9 = (bf16[2,64,128]{2,1,0:T(8,128)(2,1)S(1)}, bf16[2,64,128]{2,1,0:T(8,128)(2,1)S(1)}, u32[]{:S(2)}, u32[]{:S(2)}) collective-permute-start(bf16[2,64,128]{2,1,0:T(8,128)(2,1)S(1)} %shard_map.102.own), channel_id=1, source_target_pairs={{0,1},{1,0},{2,3},{3,2},{4,5},{5,4},{6,7},{7,6},{8,9},{9,8},{10,11... | collective-permute-start | bytes 98312 | tf_op jit(solution)/shard_map/ppermute | solution.py:37
